TPU v7x, 512 devices: a whole 4x4x16 slice. The times are simulated.
512 devices in a mesh: gx: 16 (over z_lo, core), gy: 8 (over y, z_hi), gz: 4 (over x).
Axes of the slice: x: 4, y: 4, z: 16 (z_hi: 2, z_lo: 8; z = z_hi * 8 + z_lo), core: 2. Of those that a mesh axis runs over, the one named last changes fastest.
Arguments:
- populations: float32 [27, 64, 64, 512], P(None, 'gx', 'gy', 'gz'), may hold values from 0.85 to 1.15
- coarse_populations: float32 [27, 128, 32, 256], P(None, 'gx', 'gy', 'gz'), may hold values from 0.85 to 1.15
- fluid_mask: int32 [64, 64, 512], P('gx', 'gy', 'gz'), may hold values 0 or 1
- inflow: float32 [32, 256], P('gy', 'gz'), may hold values from 0.02 to 0.08
- part_dest: int32 [16, 8, 4, 256, 1], P('gx', 'gy', 'gz'), may hold values from 0 to 15; in each aligned block of 256 rows (0 to 255, 256 to 511, ..., all dimensions but the last counted through in order) at most 32 rows name the same one
- part_cell: int32 [16, 8, 4, 256], P('gx', 'gy', 'gz'), may hold values from 0 to 2942, as said below
- part_vel: float32 [16, 8, 4, 3, 256], P('gx', 'gy', 'gz'), may hold values from -0.3 to 0.3
- part_frac: float32 [16, 8, 4, 3, 256], P('gx', 'gy', 'gz'), may hold values from 0 to 1
- part_drag: float32 [16, 8, 4, 256], P('gx', 'gy', 'gz'), may hold values from 0.05 to 0.5
Outputs:
- fine_next: float32 [27, 64, 64, 512], P(None, 'gx', 'gy', 'gz')
- coarse_next: float32 [27, 128, 32, 256], P(None, 'gx', 'gy', 'gz')
Inputs may be any that keep to these rules, and one draw needn't show every extreme that they name: `part_dest`: among the particles of one device at most 32 have the same destination. `part_cell`: ix < 3, iy < 7 and iz < 127, so that all eight corners lie in the destination block.
All inputs are finite; a program needn't handle non-finite values. No bound on the sum of `fluid_mask` on one device may be relied on, other than what follows from the above.
Results may differ from a plain program's by a relative error of at most 0.000078.
Values sent between devices are 32-bit elements; how exact they have to be, the bound alone decides.
No kernel may reach another device: no remote copies, remote signals or barrier semaphores. Data moves between devices by JAX's collectives and lax.ppermute only.
A program may use at most 128 MiB of HBM per device.

v0:
```python
import jax
import jax.numpy as jnp
from jax import lax
from jax.experimental import pallas as pl
from jax.experimental.pallas import tpu as pltpu
from jax.sharding import Mesh, PartitionSpec as P

tau_fine = 1.3
tau_coarse = 0.9
prolong_factor = (tau_fine - 1.0) / (2.0 * tau_coarse)
restrict_factor = 2.0 * (tau_coarse - 1.0) / tau_fine
stencil = [(a, b, c) for a in (-1, 0, 1) for b in (-1, 0, 1) for c in (-1, 0, 1)]
class_weight = (8.0 / 27.0, 2.0 / 27.0, 1.0 / 54.0, 1.0 / 216.0)
wall = -1e30
limit = -1e29


def moving(axis, way):
    return [i for i in range(27) if stencil[i][axis] == way]


UP = [moving(axis, 1) for axis in range(3)]
DOWN = [moving(axis, -1) for axis in range(3)]

T_VEL, T_COARSE, T_GHOST, T_FACE = 28, 31, 36, 50
X_COARSE, T_X = 80, 89

z_items = [(0, x, ch) for x in range(1, 7) for ch in range(31)]
z_items += [(0, 0, i) for i in UP[0]] + [(0, 7, i) for i in DOWN[0]]
z_deep = [(1, x, j) for x in range(1, 7) for j in range(9)]


def z_layout(way):
    inward = UP[2] if way > 0 else DOWN[2]
    items = list(z_items) + [(1, x, inward[j]) for (_, x, j) in z_deep]
    items += [(1, 0, i) for i in inward if stencil[i][0] == 1]
    items += [(1, 7, i) for i in inward if stencil[i][0] == -1]
    return {item: spot for spot, item in enumerate(items)}


def c_layout(way):
    inward = UP[2] if way > 0 else DOWN[2]
    items = [("c", x, i) for x in range(1, 9) for i in inward]
    items += [("c", 0, i) for i in inward if stencil[i][0] == 1]
    items += [("c", 9, i) for i in inward if stencil[i][0] == -1]
    items += [("g", which, i, d) for which in range(3) for i in range(27) for d in range(2)]
    items += [("i",)]
    return {item: spot for spot, item in enumerate(items)}


ZL = {1: z_layout(1), -1: z_layout(-1)}
CL = {1: c_layout(1), -1: c_layout(-1)}


def roll(value, by, axis):
    by = by % value.shape[axis]
    return value if by == 0 else pltpu.roll(value, by, axis)


def iota(shape, axis):
    return lax.broadcasted_iota(jnp.int32, shape, axis)


def dot(a, b, contract=(1, 0)):
    return lax.dot_general(
        a,
        b,
        (((contract[0],), (contract[1],)), ((), ())),
        precision=lax.Precision.HIGHEST,
        preferred_element_type=jnp.float32,
    )


def moments(n):
    totals = [n[13], None, None, None]
    parts = [[None] * 4 for _ in range(3)]
    for i in range(14, 27):
        c = stencil[i]
        k = abs(c[0]) + abs(c[1]) + abs(c[2])
        both, odd = n[i] + n[26 - i], n[i] - n[26 - i]
        totals[k] = both if totals[k] is None else totals[k] + both
        for axis in range(3):
            if c[axis]:
                have = parts[axis][k]
                if have is None:
                    parts[axis][k] = odd if c[axis] > 0 else -odd
                else:
                    parts[axis][k] = have + odd if c[axis] > 0 else have - odd
    density = sum(class_weight[k] * totals[k] for k in range(4))
    momentum = [sum(class_weight[k] * parts[axis][k] for k in (1, 2, 3)) for axis in range(3)]
    return density, momentum


def equilibrium(s, u):
    base = s - (1.5 * (u[0] * u[0] + u[1] * u[1] + u[2] * u[2])) * s
    s3, s45 = 3.0 * s, 4.5 * s
    out = [None] * 27
    out[13] = base
    for i in range(14, 27):
        cu = None
        for axis in range(3):
            c = stencil[i][axis]
            if c:
                if cu is None:
                    cu = u[axis] if c > 0 else -u[axis]
                else:
                    cu = cu + u[axis] if c > 0 else cu - u[axis]
        even, odd = base + s45 * (cu * cu), s3 * cu
        out[i], out[26 - i] = even + odd, even - odd
    return out


def collide(n, g, force, tau):
    density, m = moments(n)
    s = jnp.where(density == 0.0, 1.0, density) if g is None else density + (1.0 - g)
    inverse = 1.0 / s
    if force is not None:
        m = [m[k] + tau * force[k] for k in range(3)]
    e = equilibrium(s * (1.0 / tau), [v * inverse for v in m])
    post = [(1.0 - 1.0 / tau) * n[i] + e[i] for i in range(27)]
    return post if g is None else [jnp.where(g > 0.0, p, wall) for p in post]


def interface(n, factor):
    density, m = moments(n)
    density = jnp.where(density == 0.0, 1.0, density)
    inverse = 1.0 / density
    e = equilibrium(density, [v * inverse for v in m])
    return [e[i] + factor * (n[i] - e[i]) for i in range(27)]


S_H, S_CORE, S_ODD, S_FIRST, S_LAST, S_YLO, S_YHI, S_ZLO, S_ZHI = range(9)


def pack_kernel(sc, pop, cpop, mask, inflow, pdest, pcell, pvel, pfrac, pdrag, ymsg, outbox, vel, cc, rc, rs):
    h = sc[S_H]
    dest = pdest[...]
    onehot = (iota((16, 256), 0) == dest).astype(jnp.float32)
    earlier = (iota((256, 256), 0) < iota((256, 256), 1)).astype(jnp.bfloat16)
    before = jnp.dot(onehot.astype(jnp.bfloat16), earlier, preferred_element_type=jnp.float32)
    rank = jnp.sum(onehot * before, axis=0, keepdims=True).astype(jnp.int32)
    slot = (iota((32, 256), 0) == rank).astype(jnp.float32)
    row = iota((64, 256), 0)
    hit = (row >> 2) == dest
    odd = (row & 1) == 1
    fields = [pvel[k : k + 1, :] for k in range(3)] + [pdrag[...]]
    fields += [pfrac[k : k + 1, :] for k in range(3)] + [pcell[...].astype(jnp.float32)]
    for q in range(4):
        values = jnp.where(hit, jnp.where(odd, fields[4 + q], fields[q]), 0.0)
        outbox[:, 32 * q : 32 * q + 32] = dot(values, slot, (1, 1))
    for x in range(4):
        density, m = moments([pop[i, x] for i in range(27)])
        inverse = 1.0 / (density + (1.0 - mask[x].astype(jnp.float32)))
        for k in range(3):
            vel[k, x] = m[k] * inverse
    rc[...] = jnp.zeros(rc.shape, jnp.float32)
    for i in range(27):
        rc[i, :, 0:4, 0:64] = cpop[i]
    for x in range(8):
        post = collide([rc[i, x] for i in range(27)], None, None, tau_coarse)
        for i in range(27):
            cc[x, i] = post[i]
    pair = jnp.concatenate([pop[i, 0] + pop[i, 1] for i in range(27)], axis=0)
    narrow = ((iota((128, 128), 0) >> 1) == iota((128, 128), 1)).astype(jnp.float32)
    down, across = iota((216, 216), 0), iota((216, 216), 1)
    low = ((down >> 3) == (across >> 3)) & (((across & 7) >> 1) == (down & 7))
    mean = 0.125 * dot(low.astype(jnp.float32), dot(pair, narrow))
    settled = interface([mean[8 * i : 8 * i + 8] for i in range(27)], restrict_factor)
    for i in range(27):
        rs[i] = settled[i]
    for top in (1, 0):
        face = h if top else 1 - h
        near, third, crow, grow = (6, 5, 3, 2) if top else (0, 2, 0, 0)
        for x in range(4):
            for t in range(27):
                ymsg[face, t, 2 * x : 2 * x + 2, :] = pop[t, x, near : near + 2, :]
            ymsg[face, 27, 2 * x : 2 * x + 2, :] = mask[x, near : near + 2, :].astype(jnp.float32)
        for k in range(3):
            ymsg[face, T_VEL + k] = jnp.zeros((8, 128), jnp.float32)
            for x in range(4):
                ymsg[face, T_VEL + k, x : x + 1, :] = vel[k, x, third : third + 1, :]
        for j, i in enumerate(UP[1] if top else DOWN[1]):
            lane = 64 * (j // 5)
            for x in range(8):
                ymsg[face, T_COARSE + j % 5, x : x + 1, lane : lane + 64] = cc[x, i, crow : crow + 1, 0:64]
        ymsg[face, T_COARSE + 4, :, 64:128] = jnp.zeros((8, 64), jnp.float32)
        for t in range(14):
            ymsg[face, T_GHOST + t] = jnp.zeros((8, 128), jnp.float32)
        for t in range(27):
            lane = 64 * (t // 14)
            tile = T_GHOST + t % 14
            ymsg[face, tile, 0:2, lane : lane + 64] = rc[t, 6, grow : grow + 2, 0:64]
            ymsg[face, tile, 2:4, lane : lane + 64] = rc[t, 7, grow : grow + 2, 0:64]
            ymsg[face, tile, 4:6, lane : lane + 64] = rs[t, grow : grow + 2, 0:64]
        ymsg[face, T_GHOST + 13, 0:1, 64:128] = inflow[crow : crow + 1, :]


def particle_fields(rows):
    lane = iota((2, 128), 1) >> 5
    chunks = [[] for _ in range(4)]
    for k in range(4):
        turned = [[roll(rows[4 * k + j], 32 * s, 1) for s in range(4)] for j in range(4)]
        for q in range(4):
            value = turned[0][(0 - q) % 4]
            for j in range(1, 4):
                value = jnp.where(lane == j, turned[j][(j - q) % 4], value)
            chunks[q].append(value)
    flat = [jnp.concatenate(chunks[q], axis=1) for q in range(4)]
    return [flat[f % 4][f // 4 : f // 4 + 1, :] for f in range(8)]


def deposit(fields, velocity, xr, yr, keep):
    rows = velocity[0].shape[0]
    count = fields[0].shape[1]
    cell = fields[7].astype(jnp.int32)
    ix, iy, iz = cell >> 10, (cell >> 7) & 7, cell & 127
    fx, fy, fz = fields[4:7]
    lane = iota((128, count), 0)
    along = jnp.where(lane == iz, 1.0 - fz, jnp.where(lane == iz + 1, fz, 0.0))
    across = jnp.where(xr == ix, 1.0 - fx, jnp.where(xr == ix + 1, fx, 0.0))
    across = across * jnp.where(yr == iy, 1.0 - fy, jnp.where(yr == iy + 1, fy, 0.0))
    seen = dot(jnp.concatenate(velocity, axis=0), along)
    pushes = []
    for k in range(3):
        sampled = jnp.sum(seen[k * rows : (k + 1) * rows] * across, axis=0, keepdims=True)
        impulse = fields[3] * (fields[k] - sampled)
        pushes.append(impulse * across[0:keep])
    force = dot(jnp.concatenate(pushes, axis=0), along, (1, 1))
    return [force[k * keep : (k + 1) * keep] for k in range(3)]


def deposit_kernel(
    sc, pop, mask, vel, cc, rc, rs, inflow, near, fwd, arr, ye, xa, xb, ccy, sw, inf, hi, lo
):
    h = sc[S_H]
    lower = h == 0
    for t in range(T_FACE):
        hi[t] = jnp.where(lower, near[0, t], fwd[t])
        lo[t] = jnp.where(lower, fwd[t], near[0, t])
    own = particle_fields([arr[2 * s + h] for s in range(16)])
    partner = particle_fields([arr[2 * s + 1 - h] for s in range(16)])
    rows = []
    for s in range(16):
        tile = T_FACE + s // 2
        first, second = fwd[tile, 4 * (s % 2) : 4 * (s % 2) + 2, :], fwd[tile, 4 * (s % 2) + 2 : 4 * (s % 2) + 4, :]
        rows.append(jnp.where(lower, second, first))
    third = particle_fields(rows)
    high = [jnp.where(lower, a, b) for a, b in zip(partner, third)]
    low = [jnp.where(lower, b, a) for a, b in zip(partner, third)]
    rows32 = iota((32, 1), 0)
    force = deposit(
        own,
        [jnp.concatenate([vel[k, x] for x in range(4)], axis=0) for k in range(3)],
        rows32 >> 3,
        rows32 & 7,
        32,
    )
    rows16 = iota((16, 1), 0)
    x16 = jnp.where(rows16 < 8, rows16 >> 1, rows16 - 8)
    sides = []
    for face, fields, base, last in ((hi, high, 0, 2), (lo, low, 6, 5)):
        n = [face[i] for i in range(27)]
        g = face[27]
        density, m = moments(n)
        inverse = 1.0 / (density + (1.0 - g))
        velocity = [jnp.concatenate([m[k] * inverse, face[T_VEL + k]], axis=0) for k in range(3)]
        y16 = jnp.where(rows16 < 8, base + (rows16 & 1), last)
        f = deposit(fields, velocity, x16, y16, 8)
        sides.append(collide(n, g, f, tau_fine) + [g] + f)
    row = iota((8, 128), 0)
    for x in range(4):
        g = mask[x].astype(jnp.float32)
        f = [force[k][8 * x : 8 * x + 8] for k in range(3)]
        mine = collide([pop[i, x] for i in range(27)], g, f, tau_fine) + [g] + f
        for ch in range(31):
            ye[x, ch, 0:8, :] = mine[ch]
            ye[x, ch, 8:16, :] = jnp.where(
                row < 2,
                roll(sides[0][ch], -2 * x, 0),
                jnp.where(row >= 6, roll(sides[1][ch], 6 - 2 * x, 0), 0.0),
            )
    ccy[...] = cc[...]
    has_hi, has_lo = sc[S_YHI] == 1, sc[S_YLO] == 1
    for face, way, has, r in ((hi, DOWN[1], has_hi, 4), (lo, UP[1], has_lo, 7)):
        for j, i in enumerate(way):
            lane = 64 * (j // 5)
            for x in range(8):
                value = face[T_COARSE + j % 5, x : x + 1, lane : lane + 64]
                ccy[x, i, r : r + 1, 0:64] = jnp.where(has, value, wall)
    even = sc[S_CORE] == 0
    for ch in range(40):
        up = ye[3, ch] if ch < 31 else ye[2, UP[0][ch - 31]]
        down = ye[0, ch] if ch < 31 else ye[1, DOWN[0][ch - 31]]
        a, b = jnp.where(even, up, down), jnp.where(even, down, up)
        xa[2 * ch], xa[2 * ch + 1] = a[0:8], a[8:16]
        xb[2 * ch], xb[2 * ch + 1] = b[0:8], b[8:16]
    for j in range(9):
        up, down = ccy[7, UP[0][j]], ccy[0, DOWN[0][j]]
        xa[X_COARSE + j] = jnp.where(even, up, down)
        xb[X_COARSE + j] = jnp.where(even, down, up)
    sw[...] = jnp.zeros(sw.shape, jnp.float32)
    inf[...] = jnp.zeros((8, 128), jnp.float32)
    inf[0:4, 0:64] = inflow[...]
    inf[4:5, 0:64] = hi[T_GHOST + 13, 0:1, 64:128]
    inf[7:8, 0:64] = lo[T_GHOST + 13, 0:1, 64:128]

    @pl.when(sc[S_FIRST] == 1)
    def _():
        for t in range(27):
            lane, tile = 64 * (t // 14), T_GHOST + t % 14
            sw[t, 0:4, 0:64] = rs[t, 0:4, 0:64]
            sw[t, 4:6, 0:64] = hi[tile, 4:6, lane : lane + 64]
            sw[t, 6:8, 0:64] = lo[tile, 4:6, lane : lane + 64]

    @pl.when(sc[S_FIRST] == 0)
    def _():
        for t in range(27):
            lane, tile = 64 * (t // 14), T_GHOST + t % 14
            for part in range(2):
                to = 64 * part
                sw[t, 0:4, to : to + 64] = rc[t, 6 + part, 0:4, 0:64]
                sw[t, 4:6, to : to + 64] = hi[tile, 2 * part : 2 * part + 2, lane : lane + 64]
                sw[t, 6:8, to : to + 64] = lo[tile, 2 * part : 2 * part + 2, lane : lane + 64]


def x_tile(ye, up, down, x, ch):
    if 2 <= x <= 5:
        return ye[x - 2, ch]
    face = down if x < 2 else up
    slot = ch if x in (1, 6) else 31 + (UP[0] if x == 0 else DOWN[0]).index(ch)
    return jnp.concatenate([face(2 * slot), face(2 * slot + 1)], axis=0)


def pick(sc, index, a, b):
    even = sc[index] == 0
    return (lambda t: jnp.where(even, a[t], b[t])), (lambda t: jnp.where(even, b[t], a[t]))


def column_kernel(sc, ye, xar, xbr, swr, ccy, sw, inf, za, zb):
    up, down = pick(sc, S_CORE, xar, xbr)
    lane = iota((16, 128), 1)
    lane8 = iota((8, 128), 1)
    made = {}
    for way in (1, -1):
        tiles = [jnp.zeros((16, 128), jnp.float32) for _ in range(3)]
        for (depth, x, ch), spot in ZL[way].items():
            source = 127 - depth if way > 0 else depth
            value = roll(x_tile(ye, up, down, x, ch), spot - source, 1)
            tiles[spot // 128] = jnp.where(lane == spot % 128, value, tiles[spot // 128])
        out = [t[8 * k : 8 * k + 8] for t in tiles for k in range(2)]
        tiles = [jnp.zeros((8, 128), jnp.float32) for _ in range(2)]
        for item, spot in CL[way].items():
            if item[0] == "c":
                _, x, i = item
                if x == 0:
                    value = down(X_COARSE + UP[0].index(i))
                elif x == 9:
                    value = up(X_COARSE + DOWN[0].index(i))
                else:
                    value = ccy[x - 1, i]
                source = 63 if way > 0 else 0
            elif item[0] == "g":
                _, which, i, depth = item
                value = sw[i] if which == 2 else swr[i]
                source = (63 - depth if way > 0 else depth) + (64 if which == 1 else 0)
            else:
                value = inf[...]
                source = 63 if way > 0 else 0
            value = roll(value, spot - source, 1)
            tiles[spot // 128] = jnp.where(lane8 == spot % 128, value, tiles[spot // 128])
        made[way] = out + tiles
    even = sc[S_ODD] == 0
    for t in range(8):
        za[t] = jnp.where(even, made[1][t], made[-1][t])
        zb[t] = jnp.where(even, made[-1][t], made[1][t])


def step_kernel(
    sc, ye, xar, xbr, swr, ccy, sw, inf, zar, zbr, fine, coarse, p1, p2, gx, fx, ce, gr, late
):
    up, down = pick(sc, S_CORE, xar, xbr)
    zup, zdown = pick(sc, S_ODD, zar, zbr)
    has_yhi, has_ylo, has_zhi, has_zlo = [sc[k] == 1 for k in (S_YHI, S_YLO, S_ZHI, S_ZLO)]
    first, last = sc[S_FIRST] == 1, sc[S_LAST] == 1
    fz_up = [jnp.concatenate([zup(2 * k), zup(2 * k + 1)], axis=0) for k in range(3)]
    fz_down = [jnp.concatenate([zdown(2 * k), zdown(2 * k + 1)], axis=0) for k in range(3)]
    cz_up, cz_down = [zup(6), zup(7)], [zdown(6), zdown(7)]
    lane = iota((16, 128), 1)
    lane8 = iota((8, 128), 1)

    def side(x, ch):
        blank = wall if ch < 27 else 0.0
        value = jnp.zeros((16, 128), jnp.float32)
        for depth in range(2):
            for way, source, has, at in ((-1, fz_up, has_zhi, depth), (1, fz_down, has_zlo, 127 - depth)):
                spot = ZL[way].get((depth, x, ch))
                if spot is not None:
                    moved = jnp.where(has, roll(source[spot // 128], at - spot, 1), blank)
                    value = jnp.where(lane == at, moved, value)
        return value

    for x in range(8):
        for ch in range(31) if 0 < x < 7 else (UP[0] if x == 0 else DOWN[0]):
            main, rest = x_tile(ye, up, down, x, ch), side(x, ch)
            if ch < 27:
                to = p1.at[x, ch]
            elif ch == 27:
                to = gx.at[x - 1]
            else:
                to = fx.at[x - 1, ch - 28]
            to[:, 0:128] = main
            to[:, 128:256] = rest

    row8 = iota((8, 128), 0)
    inside = (row8 < 4) | ((row8 < 6) & has_yhi) | ((row8 >= 6) & has_ylo)
    inside = inside & (
        (lane8 < 64) | ((lane8 >= 64) & (lane8 < 66) & has_zhi) | ((lane8 >= 126) & has_zlo)
    )

    def c_side(value, up_item, down_item, blank, at=64, end=127):
        for way, source, has, item, to in ((-1, cz_up, has_zhi, up_item, at), (1, cz_down, has_zlo, down_item, end)):
            spot = CL[way].get(item)
            if spot is not None:
                moved = jnp.where(has, roll(source[spot // 128], to - spot, 1), blank)
                value = jnp.where(lane8 == to, moved, value)
        return value

    def ghost(which, i):
        value = sw[i] if which == 2 else swr[i]
        if which == 1:
            value = roll(value, 64, 1)
        value = jnp.where(lane8 < 64, value, 0.0)
        for depth in range(2):
            item = ("g", which, i, depth)
            value = c_side(value, item, item, 0.0, 64 + depth, 127 - depth)
        return value

    for x in range(8):
        for i in range(27):
            ce[x + 1, i] = c_side(ccy[x, i], ("c", x + 1, i), ("c", x + 1, i), wall)
    inflow = c_side(inf[...], ("i",), ("i",), 0.0)
    zero = jnp.zeros((8, 128), jnp.float32)
    inlet = equilibrium(jnp.ones((8, 128), jnp.float32), [inflow, zero, zero])
    for j in range(9):
        i = UP[0][j]
        came = c_side(down(X_COARSE + j), ("c", 0, i), ("c", 0, i), wall)
        ce[0, i] = jnp.where(first, jnp.where(inside, inlet[i], wall), came)
        i = DOWN[0][j]
        came = c_side(up(X_COARSE + j), ("c", 9, i), ("c", 9, i), wall)
        ce[9, i] = jnp.where(last, jnp.where(inside, ghost(0, i), wall), came)
    for i in range(27):
        a, b, c = stencil[i]
        for x in range(8):
            value = roll(roll(ce[x + 1 - a, i], b, 0), c, 1)
            value = jnp.where(value > limit, value, ce[x + 1, 26 - i])
            coarse[i, x] = value[0:4, 0:64]

    @pl.when(first)
    def _():
        n126 = [ghost(0, i) for i in range(27)]
        post = collide(n126, None, None, tau_coarse)
        for i in range(27):
            gr[0, i] = jnp.where(inside, post[i], wall)
        n127 = [ghost(1, i) for i in range(27)]
        post = collide(n127, None, None, tau_coarse)
        for i in range(27):
            gr[1, i] = jnp.where(inside, post[i], wall)
            gr[2, i] = jnp.where(inside, ghost(2, i), wall)
        later = []
        for i in range(27):
            a, b, c = stencil[i]
            value = roll(roll(gr[1 - a, i], b, 0), c, 1)
            value = jnp.where(value > limit, value, gr[1, 26 - i])
            later.append(jnp.where(inside, 0.5 * (n127[i] + value), 0.0))
        wide = ((iota((128, 256), 1) >> 1) == iota((128, 256), 0)).astype(jnp.float32)
        tall = ((iota((432, 216), 0) >> 1) == iota((432, 216), 1)).astype(jnp.float32)
        row16, lane256 = iota((16, 256), 0), iota((16, 256), 1)
        within = (row16 < 8) | ((row16 < 12) & has_yhi) | ((row16 >= 12) & has_ylo)
        within = within & (
            (lane256 < 128) | ((lane256 < 132) & has_zhi) | ((lane256 >= 252) & has_zlo)
        )
        for layer, to in ((n127, p1.at[1]), (later, late)):
            layer = interface(layer, prolong_factor)
            fines = dot(tall, dot(jnp.concatenate(layer, axis=0), wide))
            for i in range(27):
                to[i] = jnp.where(within, fines[16 * i : 16 * i + 16], wall)

    @pl.when(last)
    def _():
        for i in range(27):
            p1[6, i] = p1[5, i]

    def stream_layer(m, carry):
        g = gx[m]
        for i in range(27):
            a, b, c = stencil[i]
            value = roll(roll(p1[m + 1 - a, i], b, 0), c, 1)
            value = jnp.where(value > limit, value, p1[m + 1, 26 - i])
            p2[m, i] = jnp.where(g > 0.0, value, 0.0)
        return carry

    lax.fori_loop(0, 6, stream_layer, 0)

    def collide_layer(m, carry):
        for y in range(2):
            for z in range(2):
                rows, lanes = slice(8 * y, 8 * y + 8), slice(128 * z, 128 * z + 128)
                post = collide(
                    [p2[m, i, rows, lanes] for i in range(27)],
                    gx[m, rows, lanes],
                    [fx[m, k, rows, lanes] for k in range(3)],
                    tau_fine,
                )
                for i in range(27):
                    p2[m, i, rows, lanes] = post[i]
        return carry

    lax.fori_loop(0, 6, collide_layer, 0)

    @pl.when(first)
    def _():
        for i in range(27):
            p2[0, i] = late[i]

    @pl.when(last)
    def _():
        for i in range(27):
            p2[5, i] = p2[4, i]

    def finish_layer(x, carry):
        g = gx[x + 1, 0:8, 0:128]
        for i in range(27):
            a, b, c = stencil[i]
            value = roll(roll(p2[x + 1 - a, i], b, 0), c, 1)[0:8, 0:128]
            value = jnp.where(value > limit, value, p2[x + 1, 26 - i, 0:8, 0:128])
            fine[i, x] = jnp.where(g > 0.0, value, 0.0)
        return carry

    lax.fori_loop(0, 4, finish_layer, 0)


def f32(*shape):
    return jax.ShapeDtypeStruct(shape, jnp.float32)


def call(kernel, name, out_shape, scratch, *args):
    vmem = pl.BlockSpec(memory_space=pltpu.VMEM)
    return pl.pallas_call(
        kernel,
        out_shape=out_shape,
        in_specs=[pl.BlockSpec(memory_space=pltpu.SMEM)] + [vmem] * (len(args) - 1),
        out_specs=[vmem] * len(out_shape),
        scratch_shapes=[pltpu.VMEM(s, jnp.float32) for s in scratch],
        compiler_params=pltpu.CompilerParams(vmem_limit_bytes=40 * 1024 * 1024),
        name=name,
    )(*args)


def body(pop, cpop, mask, inflow, part_dest, part_cell, part_vel, part_frac, part_drag):
    gx, gy, h, gz = [lax.axis_index(a) for a in ("gx", "y", "h", "gz")]
    n_gx, n_y, n_gz = lax.axis_size("gx"), lax.axis_size("y"), lax.axis_size("gz")
    row = gy * 2 + h
    sc = jnp.stack(
        [
            h,
            gx % 2,
            gz % 2,
            (gx == 0).astype(jnp.int32),
            (gx == n_gx - 1).astype(jnp.int32),
            (row > 0).astype(jnp.int32),
            (row < 2 * n_y - 1).astype(jnp.int32),
            (gz > 0).astype(jnp.int32),
            (gz < n_gz - 1).astype(jnp.int32),
        ]
    ).astype(jnp.int32)
    ymsg, outbox, vel, cc, rc, rs = call(
        pack_kernel,
        "pack",
        [
            f32(2, T_FACE, 8, 128),
            f32(64, 128),
            f32(3, 4, 8, 128),
            f32(8, 27, 8, 128),
            f32(27, 8, 8, 128),
            f32(27, 8, 128),
        ],
        [],
        sc,
        pop,
        cpop,
        mask,
        inflow,
        part_dest.reshape(1, 256),
        part_cell.reshape(1, 256),
        part_vel.reshape(3, 256),
        part_frac.reshape(3, 256),
        part_drag.reshape(1, 256),
    )
    near = lax.ppermute(ymsg, "h", [(0, 1), (1, 0)])
    arr = lax.all_to_all(outbox.reshape(2 * n_gx, 2, 128), ("gx", "h"), 0, 0, tiled=True)
    onward = [(2 * y, 2 * y + 2) for y in range(n_y - 1)]
    onward += [(2 * y + 3, 2 * y + 1) for y in range(n_y - 1)]
    fwd = lax.ppermute(jnp.concatenate([near[1], arr.reshape(8, 8, 128)], axis=0), ("y", "h"), onward)
    ye, xa, xb, ccy, sw, inf = call(
        deposit_kernel,
        "deposit",
        [
            f32(4, 31, 16, 128),
            f32(T_X, 8, 128),
            f32(T_X, 8, 128),
            f32(8, 27, 8, 128),
            f32(27, 8, 128),
            f32(8, 128),
        ],
        [(T_FACE, 8, 128), (T_FACE, 8, 128)],
        sc,
        pop,
        mask,
        vel,
        cc,
        rc,
        rs,
        inflow,
        near,
        fwd,
        arr,
    )
    swr = lax.ppermute(sw, "gx", [(0, n_gx - 1), (n_gx - 1, 0)])
    xar = lax.ppermute(xa, "gx", [(i, i ^ 1) for i in range(n_gx)])
    inner = [(i, i + 1) for i in range(1, n_gx - 1, 2)]
    xbr = lax.ppermute(xb, "gx", inner + [(j, i) for i, j in inner])
    za, zb = call(
        column_kernel,
        "columns",
        [f32(8, 8, 128), f32(8, 8, 128)],
        [],
        sc,
        ye,
        xar,
        xbr,
        swr,
        ccy,
        sw,
        inf,
    )
    zar = lax.ppermute(za, "gz", [(i, i ^ 1) for i in range(n_gz)])
    inner = [(i, i + 1) for i in range(1, n_gz - 1, 2)]
    zbr = lax.ppermute(zb, "gz", inner + [(j, i) for i, j in inner])
    fine, coarse = call(
        step_kernel,
        "steps",
        [f32(27, 4, 8, 128), f32(27, 8, 4, 64)],
        [
            (8, 27, 16, 256),
            (6, 27, 16, 256),
            (6, 16, 256),
            (6, 3, 16, 256),
            (10, 27, 8, 128),
            (3, 27, 8, 128),
            (27, 16, 256),
        ],
        sc,
        ye,
        xar,
        xbr,
        swr,
        ccy,
        sw,
        inf,
        zar,
        zbr,
    )
    return fine, coarse


def solution(mesh):
    n_gx, n_gy, n_gz = [mesh.shape[a] for a in ("gx", "gy", "gz")]
    split = Mesh(mesh.devices.reshape(n_gx, n_gy // 2, 2, n_gz), ("gx", "y", "h", "gz"))
    gy = ("y", "h")
    return jax.shard_map(
        body,
        mesh=split,
        in_specs=(
            P(None, "gx", gy, "gz"),
            P(None, "gx", gy, "gz"),
            P("gx", gy, "gz"),
            P(gy, "gz"),
            P("gx", gy, "gz", None, None),
            P("gx", gy, "gz", None),
            P("gx", gy, "gz", None, None),
            P("gx", gy, "gz", None, None),
            P("gx", gy, "gz", None),
        ),
        out_specs=(P(None, "gx", gy, "gz"), P(None, "gx", gy, "gz")),
        check_vma=False,
    )
```

profile of v0, /device:TPU:28, one launch (start us, length us, event | category | flops | bytes accessed | tf_op | source)
XLA Modules:
  0.0 107.8 jit_solution(10508424139641834523)
XLA Ops:
  0.7 0.7 copy-done.9
  1.3 0.0 copy-done.8
  1.4 0.1 stack.63.sc
  1.5 0.0 copy-start.4
  1.5 0.0 copy-start.5
  1.5 0.6 copy-done.3
  2.1 0.1 copy-done.6
  2.1 0.0 copy-done.7
  2.1 0.0 copy-done.4
  2.2 0.0 copy-done.5
  2.2 1.0 copy-done
  3.2 1.0 copy-done.2
  4.2 2.5 %pack.1 = (f32[2,50,8,128]{3,2,1,0:T(8,128)S(1)}, f32[64,128]{1,0:T(8,128)}, f32[3,4,8,128]{3,2,1,0:T(8,128)S(1)}, f32[8,27,8,128]{3,2,1,0:T(8,128)S(1)}, f32[27...) custom-call(s32[9]{0:T(128)S(1)} %stack.63.sc, f32[27,4,8,128]{3,2,1,0:T(8,128)S(1)} %copy-done, ...), custom_call_target="tpu_custom_call" | custom-call | tf_op jit(solution)/shard_map/pack/pallas_call | solution.py:548
  6.8 15.7 %collective-permute-start = (f32[2,50,8,128]{3,2,1,0:T(8,128)S(1)}, f32[2,50,8,128]{3,2,1,0:T(8,128)S(1)}, u32[]{:S(2)}, u32[]{:S(2)}) collective-permute-start(f32[2,50,8,128]{3,2,1,0:T(8,128)S(1)} %get-tuple-element.20), channel_id=1, source_target_pairs={{0,4},{4,0},{1,5},{5,1},{2,6},{6,2},{3,7},{7,3},{8,12},{12,8},{9,1... | collective-permute-start | bytes 1228808 | tf_op jit(solution)/shard_map/ppermute | solution.py:599
  22.5 5.4 %all-to-all-start = ((f32[32,2,128]{2,1,0:T(2,128)}), f32[32,2,128]{2,1,0:T(2,128)S(1)}, u32[]{:S(2)}, u32[]{:S(2)}) async-start(f32[32,2,128]{2,1,0:T(2,128)} %bitcast.13), calls=%async_computation | async-start | bytes 65536 | tf_op jit(solution)/shard_map/all_to_all | solution.py:600
  27.9 0.0 copy-start.1
  27.9 8.8 %collective-permute-done.near = f32[2,50,8,128]{3,2,1,0:T(8,128)S(1)} collective-permute-done((f32[2,50,8,128]{3,2,1,0:T(8,128)S(1)}, f32[2,50,8,128]{3,2,1,0:T(8,128)S(1)}, u32[]{:S(2)}, u32[]{:S(2)}) %collective-permute-start) | collective-permute-done | bytes 409632 | tf_op jit(solution)/shard_map/ppermute | solution.py:599
  36.8 23.7 %all-to-all-done.arr = f32[32,2,128]{2,1,0:T(2,128)S(1)} async-done(((f32[32,2,128]{2,1,0:T(2,128)}), f32[32,2,128]{2,1,0:T(2,128)S(1)}, u32[]{:S(2)}, u32[]{:S(2)}) %all-to-all-start) | async-done | bytes 32800 | tf_op jit(solution)/shard_map/all_to_all | solution.py:600
  60.5 1.3 %collective-permute-start.1 = (f32[58,8,128]{2,1,0:T(8,128)S(1)}, f32[58,8,128]{2,1,0:T(8,128)S(1)}, u32[]{:S(2)}, u32[]{:S(2)}) collective-permute-start(f32[58,8,128]{2,1,0:T(8,128)S(1)} %pad_maximum_fusion), channel_id=1, source_target_pairs={{0,8},{8,16},{16,24},{12,4},{20,12},{28,20},{1,9},{9,17},{17,25},{... | collective-permute-start | bytes 712712 | tf_op jit(solution)/shard_map/ppermute | solution.py:603
  61.8 8.3 %collective-permute-done.1.fwd = f32[58,8,128]{2,1,0:T(8,128)S(1)} collective-permute-done((f32[58,8,128]{2,1,0:T(8,128)S(1)}, f32[58,8,128]{2,1,0:T(8,128)S(1)}, u32[]{:S(2)}, u32[]{:S(2)}) %collective-permute-start.1) | collective-permute-done | bytes 237600 | tf_op jit(solution)/shard_map/ppermute | solution.py:603
  70.1 2.6 %deposit.1 = (f32[4,31,16,128]{3,2,1,0:T(8,128)S(1)}, f32[89,8,128]{2,1,0:T(8,128)S(1)}, f32[89,8,128]{2,1,0:T(8,128)S(1)}, f32[8,27,8,128]{3,2,1,0:T(8,128)S(1)...) custom-call(s32[9]{0:T(128)S(1)} %stack.63.sc, f32[27,4,8,128]{3,2,1,0:T(8,128)S(1)} %copy-done.1, ...), custom_call_target="tpu_custom_call" | custom-call | tf_op jit(solution)/shard_map/deposit/pallas_call | solution.py:548
  72.7 1.9 %collective-permute-start.2 = (f32[89,8,128]{2,1,0:T(8,128)S(1)}, f32[89,8,128]{2,1,0:T(8,128)S(1)}, u32[]{:S(2)}, u32[]{:S(2)}) collective-permute-start(f32[89,8,128]{2,1,0:T(8,128)S(1)} %get-tuple-element.23), channel_id=1, source_target_pairs={{0,32},{32,0},{64,96},{96,64},{128,160},{160,128},{192,224},{224,1... | collective-permute-start | bytes 1093640 | tf_op jit(solution)/shard_map/ppermute | solution.py:629
  74.7 0.7 collective-permute-start.3
  75.4 7.8 %collective-permute-start.4 = (f32[27,8,128]{2,1,0:T(8,128)S(1)}, f32[27,8,128]{2,1,0:T(8,128)S(1)}, u32[]{:S(2)}, u32[]{:S(2)}) collective-permute-start(f32[27,8,128]{2,1,0:T(8,128)S(1)} %get-tuple-element.25.sw), channel_id=1, source_target_pairs={{0,480},{480,0},{1,481},{481,1},{2,482},{482,2},{3,483},{483,3},{4... | collective-permute-start | bytes 331784 | tf_op jit(solution)/shard_map/ppermute | solution.py:628
  83.2 6.1 %collective-permute-done.4.swr = f32[27,8,128]{2,1,0:T(8,128)S(1)} collective-permute-done((f32[27,8,128]{2,1,0:T(8,128)S(1)}, f32[27,8,128]{2,1,0:T(8,128)S(1)}, u32[]{:S(2)}, u32[]{:S(2)}) %collective-permute-start.4) | collective-permute-done | bytes 110624 | tf_op jit(solution)/shard_map/ppermute | solution.py:628
  89.3 0.0 collective-permute-done.2.xar
  89.3 2.2 %columns.1 = (f32[8,8,128]{2,1,0:T(8,128)S(1)}, f32[8,8,128]{2,1,0:T(8,128)S(1)}) custom-call(s32[9]{0:T(128)S(1)} %stack.63.sc, f32[4,31,16,128]{3,2,1,0:T(8,128)S(1)} %get-tuple-element.22.ye, f32[89,8,128]{2,1,0:T(8,128)S(1)} %collective-permute-done.2.xar, f32[89,8,128]{2,1,0:T(8,128)S(1)} %collective-permute-done.3.xbr, ...), custom_call_target="tpu_custom_call" | custom-call | tf_op jit(solution)/shard_map/columns/pallas_call | solution.py:548
  91.5 3.1 %collective-permute-start.5 = (f32[8,8,128]{2,1,0:T(8,128)S(1)}, f32[8,8,128]{2,1,0:T(8,128)S(1)}, u32[]{:S(2)}, u32[]{:S(2)}) collective-permute-start(f32[8,8,128]{2,1,0:T(8,128)S(1)} %get-tuple-element.28), channel_id=1, source_target_pairs={{0,1},{1,0},{2,3},{3,2},{4,5},{5,4},{6,7},{7,6},{8,9},{9,8},{10,11... | collective-permute-start | bytes 98312 | tf_op jit(solution)/shard_map/ppermute | solution.py:646
  94.6 1.9 %collective-permute-start.6 = (f32[8,8,128]{2,1,0:T(8,128)S(1)}, f32[8,8,128]{2,1,0:T(8,128)S(1)}, u32[]{:S(2)}, u32[]{:S(2)}) collective-permute-start(f32[8,8,128]{2,1,0:T(8,128)S(1)} %get-tuple-element.29), channel_id=1, source_target_pairs={{1,2},{2,1},{5,6},{6,5},{9,10},{10,9},{13,14},{14,13},{17,18},{18,... | collective-permute-start | bytes 98312 | tf_op jit(solution)/shard_map/ppermute | solution.py:648
  96.6 0.8 collective-permute-done.5.zar
  97.3 3.1 %collective-permute-done.6.zbr = f32[8,8,128]{2,1,0:T(8,128)S(1)} collective-permute-done((f32[8,8,128]{2,1,0:T(8,128)S(1)}, f32[8,8,128]{2,1,0:T(8,128)S(1)}, u32[]{:S(2)}, u32[]{:S(2)}) %collective-permute-start.6) | collective-permute-done | bytes 32800 | tf_op jit(solution)/shard_map/ppermute | solution.py:648
  100.4 7.3 %steps.1 = (f32[27,4,8,128]{3,2,1,0:T(8,128)}, f32[27,8,4,64]{3,2,1,0:T(4,128)}) custom-call(s32[9]{0:T(128)S(1)} %stack.63.sc, f32[4,31,16,128]{3,2,1,0:T(8,128)S(1)} %get-tuple-element.22.ye, f32[89,8,128]{2,1,0:T(8,128)S(1)} %collective-permute-done.2.xar, f32[89,8,128]{2,1,0:T(8,128)S(1)} %collective-permute-done.3.xbr, ...), custom_call_target="tpu_custom_call" | custom-call | tf_op jit(solution)/shard_map/steps/pallas_call | solution.py:548
  (12 shorter events, 0.0 us)
Async XLA Ops:
  0.7 0.7 copy-start.9
  0.7 0.7 copy-start.8
  1.4 0.7 copy-start.3
  1.4 0.7 copy-start.6
  1.4 0.7 copy-start.7
  1.5 0.7 copy-start.4
  1.5 0.7 copy-start.5
  2.2 1.0 copy-start
  3.2 1.0 copy-start.2
  6.8 30.0 %collective-permute-start = (f32[2,50,8,128]{3,2,1,0:T(8,128)S(1)}, f32[2,50,8,128]{3,2,1,0:T(8,128)S(1)}, u32[]{:S(2)}, u32[]{:S(2)}) collective-permute-start(f32[2,50,8,128]{3,2,1,0:T(8,128)S(1)} %get-tuple-element.20), channel_id=1, source_target_pairs={{0,4},{4,0},{1,5},{5,1},{2,6},{6,2},{3,7},{7,3},{8,12},{12,8},{9,1... | collective-permute-start | bytes 1228808 | tf_op jit(solution)/shard_map/ppermute | solution.py:599
  22.5 37.9 %all-to-all-start = ((f32[32,2,128]{2,1,0:T(2,128)}), f32[32,2,128]{2,1,0:T(2,128)S(1)}, u32[]{:S(2)}, u32[]{:S(2)}) async-start(f32[32,2,128]{2,1,0:T(2,128)} %bitcast.13), calls=%async_computation | async-start | bytes 65536 | tf_op jit(solution)/shard_map/all_to_all | solution.py:600
  27.9 42.2 %copy-start.1 = (f32[27,4,8,128]{3,2,1,0:T(8,128)S(1)}, f32[27,4,8,128]{3,2,1,0:T(8,128)}, u32[]{:S(2)}) copy-start(f32[27,4,8,128]{3,2,1,0:T(8,128)} %pop.3) | copy-start | bytes 1327108
  60.5 9.6 %collective-permute-start.1 = (f32[58,8,128]{2,1,0:T(8,128)S(1)}, f32[58,8,128]{2,1,0:T(8,128)S(1)}, u32[]{:S(2)}, u32[]{:S(2)}) collective-permute-start(f32[58,8,128]{2,1,0:T(8,128)S(1)} %pad_maximum_fusion), channel_id=1, source_target_pairs={{0,8},{8,16},{16,24},{12,4},{20,12},{28,20},{1,9},{9,17},{17,25},{... | collective-permute-start | bytes 712712 | tf_op jit(solution)/shard_map/ppermute | solution.py:603
  72.7 16.5 %collective-permute-start.2 = (f32[89,8,128]{2,1,0:T(8,128)S(1)}, f32[89,8,128]{2,1,0:T(8,128)S(1)}, u32[]{:S(2)}, u32[]{:S(2)}) collective-permute-start(f32[89,8,128]{2,1,0:T(8,128)S(1)} %get-tuple-element.23), channel_id=1, source_target_pairs={{0,32},{32,0},{64,96},{96,64},{128,160},{160,128},{192,224},{224,1... | collective-permute-start | bytes 1093640 | tf_op jit(solution)/shard_map/ppermute | solution.py:629
  74.7 14.6 %collective-permute-start.3 = (f32[89,8,128]{2,1,0:T(8,128)S(1)}, f32[89,8,128]{2,1,0:T(8,128)S(1)}, u32[]{:S(2)}, u32[]{:S(2)}) collective-permute-start(f32[89,8,128]{2,1,0:T(8,128)S(1)} %get-tuple-element.24), channel_id=1, source_target_pairs={{32,64},{96,128},{160,192},{224,256},{288,320},{352,384},{416,448}... | collective-permute-start | bytes 1093640 | tf_op jit(solution)/shard_map/ppermute | solution.py:631
  75.4 13.9 %collective-permute-start.4 = (f32[27,8,128]{2,1,0:T(8,128)S(1)}, f32[27,8,128]{2,1,0:T(8,128)S(1)}, u32[]{:S(2)}, u32[]{:S(2)}) collective-permute-start(f32[27,8,128]{2,1,0:T(8,128)S(1)} %get-tuple-element.25.sw), channel_id=1, source_target_pairs={{0,480},{480,0},{1,481},{481,1},{2,482},{482,2},{3,483},{483,3},{4... | collective-permute-start | bytes 331784 | tf_op jit(solution)/shard_map/ppermute | solution.py:628
  91.5 5.8 %collective-permute-start.5 = (f32[8,8,128]{2,1,0:T(8,128)S(1)}, f32[8,8,128]{2,1,0:T(8,128)S(1)}, u32[]{:S(2)}, u32[]{:S(2)}) collective-permute-start(f32[8,8,128]{2,1,0:T(8,128)S(1)} %get-tuple-element.28), channel_id=1, source_target_pairs={{0,1},{1,0},{2,3},{3,2},{4,5},{5,4},{6,7},{7,6},{8,9},{9,8},{10,11... | collective-permute-start | bytes 98312 | tf_op jit(solution)/shard_map/ppermute | solution.py:646
  94.6 5.8 %collective-permute-start.6 = (f32[8,8,128]{2,1,0:T(8,128)S(1)}, f32[8,8,128]{2,1,0:T(8,128)S(1)}, u32[]{:S(2)}, u32[]{:S(2)}) collective-permute-start(f32[8,8,128]{2,1,0:T(8,128)S(1)} %get-tuple-element.29), channel_id=1, source_target_pairs={{1,2},{2,1},{5,6},{6,5},{9,10},{10,9},{13,14},{14,13},{17,18},{18,... | collective-permute-start | bytes 98312 | tf_op jit(solution)/shard_map/ppermute | solution.py:648
where the time goes:
time: 108 us
  waiting for transfers between devices  50.8 us (47%)
  starting transfers between devices  37.9 us (35%)
  Pallas kernels  14.7 us (14%)
  local copies, waits for them, and re-layouts  3.52 us (3%)
    all_to_all x1, waiting for transfers between devices, body(): lax.all_to_all(outbox.reshape(2 * n_gx, 2, 128), ('gx', 'h'), 0, 0, tiled...  23.7 us
    ppermute x1, starting transfers between devices, body(): near = lax.ppermute(ymsg, 'h', [(0, 1), (1, 0)])  15.7 us
    pallas_call x4, Pallas kernels, call(): pl.pallas_call(kernel, out_shape=out_shape, in_specs=[pl.BlockSpec(memory...  14.7 us
    ppermute x1, waiting for transfers between devices, body(): near = lax.ppermute(ymsg, 'h', [(0, 1), (1, 0)])  8.8 us
    ppermute x1, waiting for transfers between devices, body(): lax.ppermute(jnp.concatenate([near[1], arr.reshape(8, 8, 128)], axis=0),...  8.34 us
    ppermute x1, starting transfers between devices, body(): swr = lax.ppermute(sw, 'gx', [(0, n_gx - 1), (n_gx - 1, 0)])  7.83 us
    ppermute x1, waiting for transfers between devices, body(): swr = lax.ppermute(sw, 'gx', [(0, n_gx - 1), (n_gx - 1, 0)])  6.08 us
    all_to_all x1, starting transfers between devices, body(): lax.all_to_all(outbox.reshape(2 * n_gx, 2, 128), ('gx', 'h'), 0, 0, tiled...  5.43 us
  transfers between devices with their start and end apart: 8, of which 6 were waited for; matrix products, arithmetic and copies ran while one was open for 0% of the time, Pallas kernels for 0%

commit v1 on v0

--- a/solution.py
+++ b/solution.py
@@ -22,8 +22,22 @@
 UP = [moving(axis, 1) for axis in range(3)]
 DOWN = [moving(axis, -1) for axis in range(3)]
 
-T_VEL, T_COARSE, T_GHOST, T_FACE = 28, 31, 36, 50
-X_COARSE, T_X = 80, 89
+T_DEEP, T_COARSE, T_FACE = 14, 23, 32
+X_ROWS, X_COARSE, T_X = 40, 60, 69
+
+
+def level_rows(way):
+    rows = [(ch, 0) for ch in range(46)] + [(ch, 1) for ch in range(27)]
+    rows += [(27 + j, 1) for j in range(9) if stencil[UP[0][j]][1] == way]
+    rows += [(36 + j, 1) for j in range(9) if stencil[DOWN[0][j]][1] == way]
+    spots = [(22, r, 64 * half) for r in range(4, 8) for half in range(2)]
+    spots += [(27, r, 64) for r in range(8)]
+    spots += [(t, r, 64 * half) for t in range(28, 32) for r in range(8) for half in range(2)]
+    return dict(zip(rows, spots))
+
+
+LEVEL = {1: level_rows(1), -1: level_rows(-1)}
+T_SW = 18
 
 z_items = [(0, x, ch) for x in range(1, 7) for ch in range(31)]
 z_items += [(0, 0, i) for i in UP[0]] + [(0, 7, i) for i in DOWN[0]]
@@ -43,7 +57,9 @@
     items = [("c", x, i) for x in range(1, 9) for i in inward]
     items += [("c", 0, i) for i in inward if stencil[i][0] == 1]
     items += [("c", 9, i) for i in inward if stencil[i][0] == -1]
-    items += [("g", which, i, d) for which in range(3) for i in range(27) for d in range(2)]
+    items += [("g", ch, 0) for ch in range(45)] + [("g", ch, 1) for ch in range(27)]
+    items += [("g", 27 + j, 1) for j in range(9) if stencil[UP[0][j]][2] == way]
+    items += [("g", 36 + j, 1) for j in range(9) if stencil[DOWN[0][j]][2] == way]
     items += [("i",)]
     return {item: spot for spot, item in enumerate(items)}
 
@@ -132,8 +148,8 @@
 S_H, S_CORE, S_ODD, S_FIRST, S_LAST, S_YLO, S_YHI, S_ZLO, S_ZHI = range(9)
 
 
-def pack_kernel(sc, pop, cpop, mask, inflow, pdest, pcell, pvel, pfrac, pdrag, ymsg, outbox, vel, cc, rc, rs):
-    h = sc[S_H]
+def route_kernel(sc, pdest, pcell, pvel, pfrac, pdrag, anchor, outbox):
+    del sc, anchor
     dest = pdest[...]
     onehot = (iota((16, 256), 0) == dest).astype(jnp.float32)
     earlier = (iota((256, 256), 0) < iota((256, 256), 1)).astype(jnp.bfloat16)
@@ -143,19 +159,35 @@
     row = iota((64, 256), 0)
     hit = (row >> 2) == dest
     odd = (row & 1) == 1
-    fields = [pvel[k : k + 1, :] for k in range(3)] + [pdrag[...]]
-    fields += [pfrac[k : k + 1, :] for k in range(3)] + [pcell[...].astype(jnp.float32)]
+    fields = [pvel[0, 0, 0, k : k + 1, :] for k in range(3)] + [pdrag[...]]
+    fields += [pfrac[0, 0, 0, k : k + 1, :] for k in range(3)] + [pcell[...].astype(jnp.float32)]
     for q in range(4):
         values = jnp.where(hit, jnp.where(odd, fields[4 + q], fields[q]), 0.0)
         outbox[:, 32 * q : 32 * q + 32] = dot(values, slot, (1, 1))
+
+
+def pack_kernel(
+    sc, pop_in, cpop_in, mask, inflow,
+    far, near, vel, cc, r127, rs, pop, cpop, rc, mom, faces, sems,
+):
+    h = sc[S_H]
+    copies = [pltpu.make_async_copy(pop_in, pop, sems.at[0]), pltpu.make_async_copy(cpop_in, cpop, sems.at[1])]
+    for c in copies:
+        c.start()
+    rc[...] = jnp.zeros(rc.shape, jnp.float32)
+    faces[...] = jnp.zeros(faces.shape, jnp.float32)
+    for c in copies:
+        c.wait()
     for x in range(4):
         density, m = moments([pop[i, x] for i in range(27)])
         inverse = 1.0 / (density + (1.0 - mask[x].astype(jnp.float32)))
+        mom[0, x] = density
         for k in range(3):
+            mom[k + 1, x] = m[k]
             vel[k, x] = m[k] * inverse
-    rc[...] = jnp.zeros(rc.shape, jnp.float32)
     for i in range(27):
         rc[i, :, 0:4, 0:64] = cpop[i]
+        r127[i] = rc[i, 7]
     for x in range(8):
         post = collide([rc[i, x] for i in range(27)], None, None, tau_coarse)
         for i in range(27):
@@ -166,33 +198,47 @@
     low = ((down >> 3) == (across >> 3)) & (((across & 7) >> 1) == (down & 7))
     mean = 0.125 * dot(low.astype(jnp.float32), dot(pair, narrow))
     settled = interface([mean[8 * i : 8 * i + 8] for i in range(27)], restrict_factor)
-    for i in range(27):
-        rs[i] = settled[i]
-    for top in (1, 0):
-        face = h if top else 1 - h
-        near, third, crow, grow = (6, 5, 3, 2) if top else (0, 2, 0, 0)
+    for j in range(9):
+        rs[j] = settled[DOWN[0][j]]
+    for way in (1, -1):
+        face = h if way > 0 else 1 - h
+        depths, coarse_depths = ((7, 6, 5), (3, 2)) if way > 0 else ((0, 1, 2), (0, 1))
+        inward = UP[1] if way > 0 else DOWN[1]
         for x in range(4):
-            for t in range(27):
-                ymsg[face, t, 2 * x : 2 * x + 2, :] = pop[t, x, near : near + 2, :]
-            ymsg[face, 27, 2 * x : 2 * x + 2, :] = mask[x, near : near + 2, :].astype(jnp.float32)
-        for k in range(3):
-            ymsg[face, T_VEL + k] = jnp.zeros((8, 128), jnp.float32)
-            for x in range(4):
-                ymsg[face, T_VEL + k, x : x + 1, :] = vel[k, x, third : third + 1, :]
-        for j, i in enumerate(UP[1] if top else DOWN[1]):
+
+            def put(base, k, ref, depth):
+                at = 4 * (k % 2) + x
+                value = ref[depth : depth + 1, :].astype(jnp.float32)
+                faces[face, base + k // 2, at : at + 1, :] = value
+
+            for ch in range(27):
+                put(0, ch, pop.at[ch, x], depths[0])
+            put(0, 27, mask.at[x], depths[0])
+            for k in range(9):
+                put(T_DEEP, k, pop.at[inward[k], x], depths[1])
+            for k in range(4):
+                put(T_DEEP, 9 + k, mom.at[k, x], depths[1])
+            put(T_DEEP, 13, mask.at[x], depths[1])
+            for k in range(3):
+                put(T_DEEP, 14 + k, vel.at[k, x], depths[2])
+        r = coarse_depths[0]
+        for j, i in enumerate(inward):
             lane = 64 * (j // 5)
             for x in range(8):
-                ymsg[face, T_COARSE + j % 5, x : x + 1, lane : lane + 64] = cc[x, i, crow : crow + 1, 0:64]
-        ymsg[face, T_COARSE + 4, :, 64:128] = jnp.zeros((8, 64), jnp.float32)
-        for t in range(14):
-            ymsg[face, T_GHOST + t] = jnp.zeros((8, 128), jnp.float32)
-        for t in range(27):
-            lane = 64 * (t // 14)
-            tile = T_GHOST + t % 14
-            ymsg[face, tile, 0:2, lane : lane + 64] = rc[t, 6, grow : grow + 2, 0:64]
-            ymsg[face, tile, 2:4, lane : lane + 64] = rc[t, 7, grow : grow + 2, 0:64]
-            ymsg[face, tile, 4:6, lane : lane + 64] = rs[t, grow : grow + 2, 0:64]
-        ymsg[face, T_GHOST + 13, 0:1, 64:128] = inflow[crow : crow + 1, :]
+                faces[face, T_COARSE + j % 5, x : x + 1, lane : lane + 64] = cc[x, i, r : r + 1, 0:64]
+        for (ch, depth), (tile, at, lane) in LEVEL[way].items():
+            r = coarse_depths[depth]
+            if ch < 27:
+                value = rc[ch, 7, r : r + 1, 0:64]
+            elif ch < 36:
+                value = cc[6, UP[0][ch - 27], r : r + 1, 0:64]
+            elif ch < 45:
+                value = rs[ch - 36, r : r + 1, 0:64]
+            else:
+                value = inflow[r : r + 1, :]
+            faces[face, tile, at : at + 1, lane : lane + 64] = value
+    near[0:T_FACE] = faces[0]
+    far[...] = faces[1]
 
 
 def particle_fields(rows):
@@ -229,22 +275,56 @@
     return [force[k * keep : (k + 1) * keep] for k in range(3)]
 
 
-def deposit_kernel(
-    sc, pop, mask, vel, cc, rc, rs, inflow, near, fwd, arr, ye, xa, xb, ccy, sw, inf, hi, lo
-):
+def choose(sc, near, fwd):
+    lower = sc[S_H] == 0
+    return (lambda t: jnp.where(lower, near[t], fwd[t])), (lambda t: jnp.where(lower, fwd[t], near[t]))
+
+
+def level_kernel(sc, cc, r127, rs, inflow, near, fwd, sw, inf, hi, lo):
+    up, down = choose(sc, near, fwd)
+    for t in range(22, T_FACE):
+        hi[t], lo[t] = up(t), down(t)
+    for t in range(T_SW):
+        sw[t] = jnp.zeros((8, 128), jnp.float32)
+    inf[...] = jnp.zeros((8, 128), jnp.float32)
+    inf[0:4, 0:64] = inflow[...]
+
+    def halo(ch, ref, to):
+        for face, way, rows in ((hi, -1, (4, 5)), (lo, 1, (7, 6))):
+            for depth in range(2):
+                spot = LEVEL[way].get((ch, depth))
+                if spot is not None:
+                    tile, at, lane = spot
+                    r = rows[depth]
+                    ref[r : r + 1, to : to + 64] = face[tile, at : at + 1, lane : lane + 64]
+
+    halo(45, inf, 0)
+
+    @pl.when(sc[S_FIRST] == 1)
+    def _():
+        for j in range(9):
+            to = 64 * (j % 2)
+            sw[j // 2, 0:4, to : to + 64] = rs[j, 0:4, 0:64]
+            halo(36 + j, sw.at[j // 2], to)
+
+    @pl.when(sc[S_FIRST] == 0)
+    def _():
+        for ch in range(36):
+            to = 64 * (ch % 2)
+            own = r127.at[ch] if ch < 27 else cc.at[6, UP[0][ch - 27]]
+            sw[ch // 2, 0:4, to : to + 64] = own[0:4, 0:64]
+            halo(ch, sw.at[ch // 2], to)
+
+
+def deposit_kernel(sc, pop, mask, vel, cc, near, fwd, arr, third_in, ye, xa, xb, ccy, hi, lo):
     h = sc[S_H]
     lower = h == 0
+    up, down = choose(sc, near, fwd)
     for t in range(T_FACE):
-        hi[t] = jnp.where(lower, near[0, t], fwd[t])
-        lo[t] = jnp.where(lower, fwd[t], near[0, t])
+        hi[t], lo[t] = up(t), down(t)
     own = particle_fields([arr[2 * s + h] for s in range(16)])
     partner = particle_fields([arr[2 * s + 1 - h] for s in range(16)])
-    rows = []
-    for s in range(16):
-        tile = T_FACE + s // 2
-        first, second = fwd[tile, 4 * (s % 2) : 4 * (s % 2) + 2, :], fwd[tile, 4 * (s % 2) + 2 : 4 * (s % 2) + 4, :]
-        rows.append(jnp.where(lower, second, first))
-    third = particle_fields(rows)
+    third = particle_fields([third_in[s // 4, 2 * (s % 4) : 2 * (s % 4) + 2, :] for s in range(16)])
     high = [jnp.where(lower, a, b) for a, b in zip(partner, third)]
     low = [jnp.where(lower, b, a) for a, b in zip(partner, third)]
     rows32 = iota((32, 1), 0)
@@ -255,30 +335,54 @@
         rows32 & 7,
         32,
     )
+    row = iota((8, 128), 0)
+    first_half = row < 4
+
+    def layer(base, k):
+        a, b = hi[base + k // 2], lo[base + k // 2]
+        return jnp.where(first_half, roll(a, 4, 0), b) if k % 2 else jnp.where(first_half, a, roll(b, 4, 0))
+
+    n1 = [layer(0, ch) for ch in range(27)]
+    g1 = layer(0, 27)
+    n2 = [layer(T_DEEP, k) for k in range(9)]
+    density2, m2, g2 = layer(T_DEEP, 9), [layer(T_DEEP, 10 + k) for k in range(3)], layer(T_DEEP, 13)
+    v3 = [layer(T_DEEP, 14 + k) for k in range(3)]
+    density1, m1 = moments(n1)
+    inverse1, inverse2 = 1.0 / (density1 + (1.0 - g1)), 1.0 / (density2 + (1.0 - g2))
     rows16 = iota((16, 1), 0)
-    x16 = jnp.where(rows16 < 8, rows16 >> 1, rows16 - 8)
-    sides = []
-    for face, fields, base, last in ((hi, high, 0, 2), (lo, low, 6, 5)):
-        n = [face[i] for i in range(27)]
-        g = face[27]
-        density, m = moments(n)
-        inverse = 1.0 / (density + (1.0 - g))
-        velocity = [jnp.concatenate([m[k] * inverse, face[T_VEL + k]], axis=0) for k in range(3)]
-        y16 = jnp.where(rows16 < 8, base + (rows16 & 1), last)
-        f = deposit(fields, velocity, x16, y16, 8)
-        sides.append(collide(n, g, f, tau_fine) + [g] + f)
-    row = iota((8, 128), 0)
+    pushed = []
+    for above, fields in ((True, high), (False, low)):
+        velocity = []
+        for k in range(3):
+            a, b = m1[k] * inverse1, m2[k] * inverse2
+            c = jnp.where(first_half, v3[k] if above else roll(v3[k], 4, 0), 0.0)
+            ab = jnp.where(first_half, a, roll(b, 4, 0)) if above else jnp.where(first_half, roll(a, 4, 0), b)
+            velocity.append(jnp.concatenate([ab, c], axis=0))
+        depth = rows16 >> 2
+        pushed.append(deposit(fields, velocity, rows16 & 3, depth if above else 7 - depth, 8))
+    f1 = [jnp.where(first_half, a, roll(b, 4, 0)) for a, b in zip(*pushed)]
+    f2 = [jnp.where(first_half, roll(a, 4, 0), b) for a, b in zip(*pushed)]
+    side1 = collide(n1, g1, f1, tau_fine) + [g1] + f1
+    s2 = density2 + (1.0 - g2)
+    u2 = [(m2[k] + tau_fine * f2[k]) * inverse2 for k in range(3)]
+    u2[1] = jnp.where(first_half, u2[1], -u2[1])
+    e2 = equilibrium(s2 * (1.0 / tau_fine), u2)
+    side2 = [
+        jnp.where(g2 > 0.0, (1.0 - 1.0 / tau_fine) * n2[k] + e2[DOWN[1][k]], wall) for k in range(9)
+    ]
     for x in range(4):
         g = mask[x].astype(jnp.float32)
         f = [force[k][8 * x : 8 * x + 8] for k in range(3)]
         mine = collide([pop[i, x] for i in range(27)], g, f, tau_fine) + [g] + f
         for ch in range(31):
             ye[x, ch, 0:8, :] = mine[ch]
-            ye[x, ch, 8:16, :] = jnp.where(
-                row < 2,
-                roll(sides[0][ch], -2 * x, 0),
-                jnp.where(row >= 6, roll(sides[1][ch], 6 - 2 * x, 0), 0.0),
-            )
+            value = jnp.where(row == 0, roll(side1[ch], -x, 0), 0.0)
+            value = jnp.where(row == 7, roll(side1[ch], 3 - x, 0), value)
+            if ch in DOWN[1]:
+                value = jnp.where(row == 1, roll(side2[DOWN[1].index(ch)], 1 - x, 0), value)
+            if ch in UP[1]:
+                value = jnp.where(row == 6, roll(side2[UP[1].index(ch)], 2 - x, 0), value)
+            ye[x, ch, 8:16, :] = value
     ccy[...] = cc[...]
     has_hi, has_lo = sc[S_YHI] == 1, sc[S_YLO] == 1
     for face, way, has, r in ((hi, DOWN[1], has_hi, 4), (lo, UP[1], has_lo, 7)):
@@ -288,39 +392,24 @@
                 value = face[T_COARSE + j % 5, x : x + 1, lane : lane + 64]
                 ccy[x, i, r : r + 1, 0:64] = jnp.where(has, value, wall)
     even = sc[S_CORE] == 0
-    for ch in range(40):
-        up = ye[3, ch] if ch < 31 else ye[2, UP[0][ch - 31]]
-        down = ye[0, ch] if ch < 31 else ye[1, DOWN[0][ch - 31]]
-        a, b = jnp.where(even, up, down), jnp.where(even, down, up)
-        xa[2 * ch], xa[2 * ch + 1] = a[0:8], a[8:16]
-        xb[2 * ch], xb[2 * ch + 1] = b[0:8], b[8:16]
+    outer = (row < 2) | (row >= 6)
+
+    def send(t, a, b):
+        xa[t], xb[t] = jnp.where(even, a, b), jnp.where(even, b, a)
+
+    ups = [(3, ch) for ch in range(31)] + [(2, i) for i in UP[0]]
+    downs = [(0, ch) for ch in range(31)] + [(1, i) for i in DOWN[0]]
+    for k in range(40):
+        send(k, ye[ups[k] + (slice(0, 8),)], ye[downs[k] + (slice(0, 8),)])
+    for k in range(20):
+        pairs = []
+        for which in (ups, downs):
+            first, second = which[2 * k], which[2 * k + 1]
+            value = roll(ye[second + (slice(8, 16),)], 4, 0)
+            pairs.append(jnp.where(outer, ye[first + (slice(8, 16),)], value))
+        send(X_ROWS + k, *pairs)
     for j in range(9):
-        up, down = ccy[7, UP[0][j]], ccy[0, DOWN[0][j]]
-        xa[X_COARSE + j] = jnp.where(even, up, down)
-        xb[X_COARSE + j] = jnp.where(even, down, up)
-    sw[...] = jnp.zeros(sw.shape, jnp.float32)
-    inf[...] = jnp.zeros((8, 128), jnp.float32)
-    inf[0:4, 0:64] = inflow[...]
-    inf[4:5, 0:64] = hi[T_GHOST + 13, 0:1, 64:128]
-    inf[7:8, 0:64] = lo[T_GHOST + 13, 0:1, 64:128]
-
-    @pl.when(sc[S_FIRST] == 1)
-    def _():
-        for t in range(27):
-            lane, tile = 64 * (t // 14), T_GHOST + t % 14
-            sw[t, 0:4, 0:64] = rs[t, 0:4, 0:64]
-            sw[t, 4:6, 0:64] = hi[tile, 4:6, lane : lane + 64]
-            sw[t, 6:8, 0:64] = lo[tile, 4:6, lane : lane + 64]
-
-    @pl.when(sc[S_FIRST] == 0)
-    def _():
-        for t in range(27):
-            lane, tile = 64 * (t // 14), T_GHOST + t % 14
-            for part in range(2):
-                to = 64 * part
-                sw[t, 0:4, to : to + 64] = rc[t, 6 + part, 0:4, 0:64]
-                sw[t, 4:6, to : to + 64] = hi[tile, 2 * part : 2 * part + 2, lane : lane + 64]
-                sw[t, 6:8, to : to + 64] = lo[tile, 2 * part : 2 * part + 2, lane : lane + 64]
+        send(X_COARSE + j, ccy[7, UP[0][j]], ccy[0, DOWN[0][j]])
 
 
 def x_tile(ye, up, down, x, ch):
@@ -328,7 +417,9 @@
         return ye[x - 2, ch]
     face = down if x < 2 else up
     slot = ch if x in (1, 6) else 31 + (UP[0] if x == 0 else DOWN[0]).index(ch)
-    return jnp.concatenate([face(2 * slot), face(2 * slot + 1)], axis=0)
+    row = iota((8, 128), 0)
+    rest = roll(face(X_ROWS + slot // 2), 4 * (slot % 2), 0)
+    return jnp.concatenate([face(slot), jnp.where((row < 2) | (row >= 6), rest, 0.0)], axis=0)
 
 
 def pick(sc, index, a, b):
@@ -360,9 +451,10 @@
                     value = ccy[x - 1, i]
                 source = 63 if way > 0 else 0
             elif item[0] == "g":
-                _, which, i, depth = item
-                value = sw[i] if which == 2 else swr[i]
-                source = (63 - depth if way > 0 else depth) + (64 if which == 1 else 0)
+                _, ch, depth = item
+                q = ch if ch < 36 else ch - 36
+                value = swr[q // 2] if ch < 36 else sw[q // 2]
+                source = (63 - depth if way > 0 else depth) + 64 * (q % 2)
             else:
                 value = inf[...]
                 source = 63 if way > 0 else 0
@@ -425,13 +517,11 @@
                 value = jnp.where(lane8 == to, moved, value)
         return value
 
-    def ghost(which, i):
-        value = sw[i] if which == 2 else swr[i]
-        if which == 1:
-            value = roll(value, 64, 1)
+    def ghost(ch, ref, q):
+        value = roll(ref[q // 2], 64 * (q % 2), 1)
         value = jnp.where(lane8 < 64, value, 0.0)
         for depth in range(2):
-            item = ("g", which, i, depth)
+            item = ("g", ch, depth)
             value = c_side(value, item, item, 0.0, 64 + depth, 127 - depth)
         return value
 
@@ -447,7 +537,7 @@
         ce[0, i] = jnp.where(first, jnp.where(inside, inlet[i], wall), came)
         i = DOWN[0][j]
         came = c_side(up(X_COARSE + j), ("c", 9, i), ("c", 9, i), wall)
-        ce[9, i] = jnp.where(last, jnp.where(inside, ghost(0, i), wall), came)
+        ce[9, i] = jnp.where(last, jnp.where(inside, ghost(j, swr, j), wall), came)
     for i in range(27):
         a, b, c = stencil[i]
         for x in range(8):
@@ -457,15 +547,13 @@
 
     @pl.when(first)
     def _():
-        n126 = [ghost(0, i) for i in range(27)]
-        post = collide(n126, None, None, tau_coarse)
-        for i in range(27):
-            gr[0, i] = jnp.where(inside, post[i], wall)
-        n127 = [ghost(1, i) for i in range(27)]
+        n127 = [ghost(i, swr, i) for i in range(27)]
         post = collide(n127, None, None, tau_coarse)
         for i in range(27):
             gr[1, i] = jnp.where(inside, post[i], wall)
-            gr[2, i] = jnp.where(inside, ghost(2, i), wall)
+        for j in range(9):
+            gr[0, UP[0][j]] = jnp.where(inside, ghost(27 + j, swr, 27 + j), wall)
+            gr[2, DOWN[0][j]] = jnp.where(inside, ghost(36 + j, sw, j), wall)
         later = []
         for i in range(27):
             a, b, c = stencil[i]
@@ -543,15 +631,18 @@
     return jax.ShapeDtypeStruct(shape, jnp.float32)
 
 
-def call(kernel, name, out_shape, scratch, *args):
+def call(kernel, name, out_shape, scratch, *args, held=0, cost=0):
     vmem = pl.BlockSpec(memory_space=pltpu.VMEM)
+    raw = pl.BlockSpec(memory_space=pltpu.HBM)
     return pl.pallas_call(
         kernel,
         out_shape=out_shape,
-        in_specs=[pl.BlockSpec(memory_space=pltpu.SMEM)] + [vmem] * (len(args) - 1),
+        in_specs=[pl.BlockSpec(memory_space=pltpu.SMEM)] + [raw] * held + [vmem] * (len(args) - 1 - held),
         out_specs=[vmem] * len(out_shape),
-        scratch_shapes=[pltpu.VMEM(s, jnp.float32) for s in scratch],
+        scratch_shapes=[pltpu.VMEM(s, jnp.float32) for s in scratch]
+        + ([pltpu.SemaphoreType.DMA((held,))] if held else []),
         compiler_params=pltpu.CompilerParams(vmem_limit_bytes=40 * 1024 * 1024),
+        cost_estimate=pl.CostEstimate(flops=cost, bytes_accessed=1, transcendentals=0) if cost else None,
         name=name,
     )(*args)
 
@@ -573,59 +664,78 @@
             (gz < n_gz - 1).astype(jnp.int32),
         ]
     ).astype(jnp.int32)
-    ymsg, outbox, vel, cc, rc, rs = call(
+    far, near, vel, cc, r127, rs = call(
         pack_kernel,
         "pack",
         [
-            f32(2, T_FACE, 8, 128),
-            f32(64, 128),
+            f32(T_FACE, 8, 128),
+            f32(T_FACE + 1, 8, 128),
             f32(3, 4, 8, 128),
             f32(8, 27, 8, 128),
-            f32(27, 8, 8, 128),
             f32(27, 8, 128),
+            f32(9, 8, 128),
         ],
-        [],
+        [(27, 4, 8, 128), (27, 8, 4, 64), (27, 8, 8, 128), (4, 4, 8, 128), (2, T_FACE, 8, 128)],
         sc,
         pop,
         cpop,
         mask,
         inflow,
+        held=2,
+        cost=1_000_000_000,
+    )
+    (outbox,) = call(
+        route_kernel,
+        "route",
+        [f32(64, 128)],
+        [],
+        sc,
         part_dest.reshape(1, 256),
         part_cell.reshape(1, 256),
-        part_vel.reshape(3, 256),
-        part_frac.reshape(3, 256),
+        part_vel,
+        part_frac,
         part_drag.reshape(1, 256),
-    )
-    near = lax.ppermute(ymsg, "h", [(0, 1), (1, 0)])
+        rs,
+        cost=50_000_000_000,
+    )
+    far = lax.ppermute(far, "h", [(0, 1), (1, 0)])
     arr = lax.all_to_all(outbox.reshape(2 * n_gx, 2, 128), ("gx", "h"), 0, 0, tiled=True)
+    near = lax.ppermute(near, "h", [(0, 1), (1, 0)])
     onward = [(2 * y, 2 * y + 2) for y in range(n_y - 1)]
     onward += [(2 * y + 3, 2 * y + 1) for y in range(n_y - 1)]
-    fwd = lax.ppermute(jnp.concatenate([near[1], arr.reshape(8, 8, 128)], axis=0), ("y", "h"), onward)
-    ye, xa, xb, ccy, sw, inf = call(
+    partner = jnp.where(h == 0, arr[1::2], arr[0::2]).reshape(4, 8, 128)
+    fwd = lax.ppermute(far, ("y", "h"), onward)
+    third = lax.ppermute(partner, ("y", "h"), onward)
+    sw, inf = call(
+        level_kernel,
+        "level",
+        [f32(T_X + 1, 8, 128), f32(8, 128)],
+        [(T_FACE, 8, 128), (T_FACE, 8, 128)],
+        sc,
+        cc,
+        r127,
+        rs,
+        inflow,
+        near,
+        fwd,
+    )
+    swr = lax.ppermute(sw, "gx", [(0, n_gx - 1), (n_gx - 1, 0)])
+    ye, xa, xb, ccy = call(
         deposit_kernel,
         "deposit",
-        [
-            f32(4, 31, 16, 128),
-            f32(T_X, 8, 128),
-            f32(T_X, 8, 128),
-            f32(8, 27, 8, 128),
-            f32(27, 8, 128),
-            f32(8, 128),
-        ],
+        [f32(4, 31, 16, 128), f32(T_X, 8, 128), f32(T_X, 8, 128), f32(8, 27, 8, 128)],
         [(T_FACE, 8, 128), (T_FACE, 8, 128)],
         sc,
         pop,
         mask,
         vel,
         cc,
-        rc,
-        rs,
-        inflow,
         near,
         fwd,
         arr,
-    )
-    swr = lax.ppermute(sw, "gx", [(0, n_gx - 1), (n_gx - 1, 0)])
+        third,
+        cost=50_000_000_000,
+    )
     xar = lax.ppermute(xa, "gx", [(i, i ^ 1) for i in range(n_gx)])
     inner = [(i, i + 1) for i in range(1, n_gx - 1, 2)]
     xbr = lax.ppermute(xb, "gx", inner + [(j, i) for i, j in inner])

time: 108 us -> 88.3 us (0.82)
  the two profiles are of different devices: /device:TPU:28 before, /device:TPU:508 now
where the time goes in v1:
time: 88.3 us; the launch traced here: 87.7 us
  starting transfers between devices  50.1 us (57%)
  waiting for transfers between devices  18.1 us (20%)
  Pallas kernels  15.2 us (17%)
  local copies, waits for them, and re-layouts  3.4 us (4%)
  between operations  0.91 us (1%)
    pallas_call x6, Pallas kernels, call(): pl.pallas_call(kernel, out_shape=out_shape, in_specs=[pl.BlockSpec(memory...  15.2 us
    ppermute x1, starting transfers between devices, body(): xar = lax.ppermute(xa, 'gx', [(i, i ^ 1) for i in range(n_gx)])  12.8 us
    ppermute x1, starting transfers between devices, body(): near = lax.ppermute(near, 'h', [(0, 1), (1, 0)])  9.97 us
    all_to_all x1, starting transfers between devices, body(): lax.all_to_all(outbox.reshape(2 * n_gx, 2, 128), ('gx', 'h'), 0, 0, tiled...  8.39 us
    ppermute x1, waiting for transfers between devices, body(): near = lax.ppermute(near, 'h', [(0, 1), (1, 0)])  8.23 us
    ppermute x1, starting transfers between devices, body(): far = lax.ppermute(far, 'h', [(0, 1), (1, 0)])  6.34 us
    ppermute x1, waiting for transfers between devices, body(): xbr = lax.ppermute(xb, 'gx', inner + [(j, i) for i, j in inner])  5.97 us
    unnamed x22, local copies, waits for them, and re-layouts  3.31 us
  transfers between devices with their start and end apart: 10, of which 4 were waited for; matrix products, arithmetic and copies ran while one was open for 0% of the time, Pallas kernels for 6%

profile of v1, /device:TPU:508, one launch (start us, length us, event | category | flops | bytes accessed | tf_op | source)
XLA Modules:
  0.0 87.7 jit_solution(5870205988552164710)
XLA Ops:
  0.7 0.1 stack.63.sc
  0.8 0.6 copy-done.4
  1.4 1.0 %copy-done.1 = f32[27,8,4,64]{3,2,1,0:T(4,128)S(1)} copy-done((f32[27,8,4,64]{3,2,1,0:T(4,128)S(1)}, f32[27,8,4,64]{3,2,1,0:T(4,128)}, u32[]{:S(2)}) %copy-start.1) | copy-done | bytes 221208
  2.4 1.0 %copy-done.2 = f32[27,4,8,128]{3,2,1,0:T(8,128)S(1)} copy-done((f32[27,4,8,128]{3,2,1,0:T(8,128)S(1)}, f32[27,4,8,128]{3,2,1,0:T(8,128)}, u32[]{:S(2)}) %copy-start.2) | copy-done | bytes 442392
  3.4 2.6 %pack.1 = (f32[32,8,128]{2,1,0:T(8,128)S(1)}, f32[33,8,128]{2,1,0:T(8,128)S(1)}, f32[3,4,8,128]{3,2,1,0:T(8,128)S(1)}, f32[8,27,8,128]{3,2,1,0:T(8,128)S(1)}, f3...) custom-call(s32[9]{0:T(128)S(1)} %stack.63.sc, f32[27,4,8,128]{3,2,1,0:T(8,128)S(1)} %copy-done.2, ...), custom_call_target="tpu_custom_call" | custom-call | flops 1000000000 | bytes 1 | tf_op jit(solution)/shard_map/pack/pallas_call | solution.py:637
  6.1 0.0 copy-start.9
  6.1 6.3 %collective-permute-start.1 = (f32[32,8,128]{2,1,0:T(8,128)S(1)}, f32[32,8,128]{2,1,0:T(8,128)S(1)}, u32[]{:S(2)}, u32[]{:S(2)}) collective-permute-start(f32[32,8,128]{2,1,0:T(8,128)S(1)} %get-tuple-element.19), channel_id=1, source_target_pairs={{0,4},{4,0},{1,5},{5,1},{2,6},{6,2},{3,7},{7,3},{8,12},{12,8},{9,1... | collective-permute-start | bytes 393224 | tf_op jit(solution)/shard_map/ppermute | solution.py:701
  12.5 0.0 copy-start.5
  12.5 0.7 copy-done.5
  13.1 1.8 %route.1 = f32[64,128]{1,0:T(8,128)} custom-call(s32[9]{0:T(128)S(1)} %stack.63.sc, s32[1,256]{1,0:T(1,128)S(1)} %bitcast.14, s32[1,256]{1,0:T(1,128)S(1)} %bitcast.15, f32[1,1,1,3,256]{4,3,2,1,0:T(4,128)S(1)} %copy.11.pvel, f32[1,1,1,3,256]{4,3,2,1,0:T(4,128)S(1)} %copy.12.pfrac, f32[1,256]{1,0:T(1,128)S(1)} %bitcast.16, ...), custom_call_target="tpu_custom_call" | custom-call | flops 49999998976 | bytes 1 | tf_op jit(solution)/shard_map/route/pallas_call | solution.py:637
  14.9 8.4 %all-to-all-start = ((f32[32,2,128]{2,1,0:T(2,128)}), f32[32,2,128]{2,1,0:T(2,128)S(1)}, u32[]{:S(2)}, u32[]{:S(2)}) async-start(f32[32,2,128]{2,1,0:T(2,128)} %bitcast.12), calls=%async_computation | async-start | bytes 65536 | tf_op jit(solution)/shard_map/all_to_all | solution.py:702
  23.3 10.0 %collective-permute-start = (f32[33,8,128]{2,1,0:T(8,128)S(1)}, f32[33,8,128]{2,1,0:T(8,128)S(1)}, u32[]{:S(2)}, u32[]{:S(2)}) collective-permute-start(f32[33,8,128]{2,1,0:T(8,128)S(1)} %get-tuple-element.18), channel_id=1, source_target_pairs={{0,4},{4,0},{1,5},{5,1},{2,6},{6,2},{3,7},{7,3},{8,12},{12,8},{9,1... | collective-permute-start | bytes 405512 | tf_op jit(solution)/shard_map/ppermute | solution.py:703
  33.3 0.0 collective-permute-done.1
  33.3 2.7 %collective-permute-start.2 = (f32[32,8,128]{2,1,0:T(8,128)S(1)}, f32[32,8,128]{2,1,0:T(8,128)S(1)}, u32[]{:S(2)}, u32[]{:S(2)}) collective-permute-start(f32[32,8,128]{2,1,0:T(8,128)S(1)} %collective-permute-done.1), channel_id=1, source_target_pairs={{0,8},{8,16},{16,24},{12,4},{20,12},{28,20},{1,9},{9,17},{17,25},{... | collective-permute-start | bytes 393224 | tf_op jit(solution)/shard_map/ppermute | solution.py:707
  35.9 0.0 all-to-all-done.arr
  36.0 2.4 %collective-permute-start.3 = (f32[4,8,128]{2,1,0:T(8,128)S(1)}, f32[4,8,128]{2,1,0:T(8,128)S(1)}, u32[]{:S(2)}, u32[]{:S(2)}) collective-permute-start(f32[4,8,128]{2,1,0:T(8,128)S(1)} %bitcast.17), channel_id=1, source_target_pairs={{0,8},{8,16},{16,24},{12,4},{20,12},{28,20},{1,9},{9,17},{17,25},{... | collective-permute-start | bytes 49160 | tf_op jit(solution)/shard_map/ppermute | solution.py:708
  38.3 8.2 %collective-permute-done.near = f32[33,8,128]{2,1,0:T(8,128)S(1)} collective-permute-done((f32[33,8,128]{2,1,0:T(8,128)S(1)}, f32[33,8,128]{2,1,0:T(8,128)S(1)}, u32[]{:S(2)}, u32[]{:S(2)}) %collective-permute-start) | collective-permute-done | bytes 135200 | tf_op jit(solution)/shard_map/ppermute | solution.py:703
  46.6 0.0 collective-permute-done.2.fwd
  46.6 0.7 level.1
  47.3 0.7 collective-permute-start.6
  48.0 0.0 collective-permute-done.3.third_in
  48.0 2.5 %deposit.1 = (f32[4,31,16,128]{3,2,1,0:T(8,128)S(1)}, f32[69,8,128]{2,1,0:T(8,128)S(1)}, f32[69,8,128]{2,1,0:T(8,128)S(1)}, f32[8,27,8,128]{3,2,1,0:T(8,128)S(1)}) custom-call(s32[9]{0:T(128)S(1)} %stack.63.sc, f32[27,4,8,128]{3,2,1,0:T(8,128)S(1)} %copy-done.3, s32[4,8,128]{2,1,0:T(8,128)S(1)} %copy-done.4, f32[3,4,8,128]{3,2,1,0:T(8,128)S(1)} %get-tuple-element.16.vel, ...), custom_call_target="tpu_custom_call" | custom-call | flops 49999998976 | bytes 1 | tf_op jit(solution)/shard_map/deposit/pallas_call | solution.py:637
  50.5 12.8 %collective-permute-start.4 = (f32[69,8,128]{2,1,0:T(8,128)S(1)}, f32[69,8,128]{2,1,0:T(8,128)S(1)}, u32[]{:S(2)}, u32[]{:S(2)}) collective-permute-start(f32[69,8,128]{2,1,0:T(8,128)S(1)} %get-tuple-element.22), channel_id=1, source_target_pairs={{0,32},{32,0},{64,96},{96,64},{128,160},{160,128},{192,224},{224,1... | collective-permute-start | bytes 847880 | tf_op jit(solution)/shard_map/ppermute | solution.py:739
  63.3 1.9 %collective-permute-start.5 = (f32[69,8,128]{2,1,0:T(8,128)S(1)}, f32[69,8,128]{2,1,0:T(8,128)S(1)}, u32[]{:S(2)}, u32[]{:S(2)}) collective-permute-start(f32[69,8,128]{2,1,0:T(8,128)S(1)} %get-tuple-element.23), channel_id=1, source_target_pairs={{32,64},{96,128},{160,192},{224,256},{288,320},{352,384},{416,448}... | collective-permute-start | bytes 847880 | tf_op jit(solution)/shard_map/ppermute | solution.py:741
  65.3 6.0 %collective-permute-done.5.xbr = f32[69,8,128]{2,1,0:T(8,128)S(1)} collective-permute-done((f32[69,8,128]{2,1,0:T(8,128)S(1)}, f32[69,8,128]{2,1,0:T(8,128)S(1)}, u32[]{:S(2)}, u32[]{:S(2)}) %collective-permute-start.5) | collective-permute-done | bytes 282656 | tf_op jit(solution)/shard_map/ppermute | solution.py:741
  71.3 0.0 collective-permute-done.6.swr
  71.3 2.1 %columns.1 = (f32[8,8,128]{2,1,0:T(8,128)S(1)}, f32[8,8,128]{2,1,0:T(8,128)S(1)}) custom-call(s32[9]{0:T(128)S(1)} %stack.63.sc, f32[4,31,16,128]{3,2,1,0:T(8,128)S(1)} %get-tuple-element.21.ye, f32[69,8,128]{2,1,0:T(8,128)S(1)} %collective-permute-done.4.xar, f32[69,8,128]{2,1,0:T(8,128)S(1)} %collective-permute-done.5.xbr, ...), custom_call_target="tpu_custom_call" | custom-call | tf_op jit(solution)/shard_map/columns/pallas_call | solution.py:637
  73.3 3.1 %collective-permute-start.7 = (f32[8,8,128]{2,1,0:T(8,128)S(1)}, f32[8,8,128]{2,1,0:T(8,128)S(1)}, u32[]{:S(2)}, u32[]{:S(2)}) collective-permute-start(f32[8,8,128]{2,1,0:T(8,128)S(1)} %get-tuple-element.28), channel_id=1, source_target_pairs={{0,1},{1,0},{2,3},{3,2},{4,5},{5,4},{6,7},{7,6},{8,9},{9,8},{10,11... | collective-permute-start | bytes 98312 | tf_op jit(solution)/shard_map/ppermute | solution.py:756
  76.5 1.9 %collective-permute-start.8 = (f32[8,8,128]{2,1,0:T(8,128)S(1)}, f32[8,8,128]{2,1,0:T(8,128)S(1)}, u32[]{:S(2)}, u32[]{:S(2)}) collective-permute-start(f32[8,8,128]{2,1,0:T(8,128)S(1)} %get-tuple-element.29), channel_id=1, source_target_pairs={{1,2},{2,1},{5,6},{6,5},{9,10},{10,9},{13,14},{14,13},{17,18},{18,... | collective-permute-start | bytes 98312 | tf_op jit(solution)/shard_map/ppermute | solution.py:758
  78.4 0.8 collective-permute-done.7.zar
  79.2 3.1 %collective-permute-done.8.zbr = f32[8,8,128]{2,1,0:T(8,128)S(1)} collective-permute-done((f32[8,8,128]{2,1,0:T(8,128)S(1)}, f32[8,8,128]{2,1,0:T(8,128)S(1)}, u32[]{:S(2)}, u32[]{:S(2)}) %collective-permute-start.8) | collective-permute-done | bytes 32800 | tf_op jit(solution)/shard_map/ppermute | solution.py:758
  82.3 5.5 %steps.1 = (f32[27,4,8,128]{3,2,1,0:T(8,128)}, f32[27,8,4,64]{3,2,1,0:T(4,128)}) custom-call(s32[9]{0:T(128)S(1)} %stack.63.sc, f32[4,31,16,128]{3,2,1,0:T(8,128)S(1)} %get-tuple-element.21.ye, f32[69,8,128]{2,1,0:T(8,128)S(1)} %collective-permute-done.4.xar, f32[69,8,128]{2,1,0:T(8,128)S(1)} %collective-permute-done.5.xbr, ...), custom_call_target="tpu_custom_call" | custom-call | tf_op jit(solution)/shard_map/steps/pallas_call | solution.py:637
  (18 shorter events, 0.0 us)
Async XLA Ops:
  0.7 0.7 copy-start.4
  0.7 0.7 copy-start
  1.4 1.0 %copy-start.1 = (f32[27,8,4,64]{3,2,1,0:T(4,128)S(1)}, f32[27,8,4,64]{3,2,1,0:T(4,128)}, u32[]{:S(2)}) copy-start(f32[27,8,4,64]{3,2,1,0:T(4,128)} %cpop_in.1) | copy-start | bytes 663556
  2.4 1.0 %copy-start.2 = (f32[27,4,8,128]{3,2,1,0:T(8,128)S(1)}, f32[27,4,8,128]{3,2,1,0:T(8,128)}, u32[]{:S(2)}) copy-start(f32[27,4,8,128]{3,2,1,0:T(8,128)} %pop.1) | copy-start | bytes 1327108
  3.4 9.0 %copy-start.8 = (f32[1,1,1,3,256]{4,2,3,1,0:T(1,128)S(1)}, f32[1,1,1,3,256]{4,2,3,1,0:T(1,128)}, u32[]{:S(2)}) copy-start(f32[1,1,1,3,256]{4,2,3,1,0:T(1,128)} %param.15) | copy-start | bytes 9220
  3.4 9.1 %copy-start.6 = (s32[1,1,1,256]{3,2,1,0:T(1,128)S(1)}, s32[1,1,1,256]{3,2,1,0:T(1,128)}, u32[]{:S(2)}) copy-start(s32[1,1,1,256]{3,2,1,0:T(1,128)} %param.14) | copy-start | bytes 3076
  3.4 9.1 %copy-start.7 = (f32[1,1,1,256]{3,2,1,0:T(1,128)S(1)}, f32[1,1,1,256]{3,2,1,0:T(1,128)}, u32[]{:S(2)}) copy-start(f32[1,1,1,256]{3,2,1,0:T(1,128)} %param.17) | copy-start | bytes 3076
  6.1 6.4 %copy-start.9 = (f32[1,1,1,3,256]{4,2,3,1,0:T(1,128)S(1)}, f32[1,1,1,3,256]{4,2,3,1,0:T(1,128)}, u32[]{:S(2)}) copy-start(f32[1,1,1,3,256]{4,2,3,1,0:T(1,128)} %param.16) | copy-start | bytes 9220
  6.1 27.2 %collective-permute-start.1 = (f32[32,8,128]{2,1,0:T(8,128)S(1)}, f32[32,8,128]{2,1,0:T(8,128)S(1)}, u32[]{:S(2)}, u32[]{:S(2)}) collective-permute-start(f32[32,8,128]{2,1,0:T(8,128)S(1)} %get-tuple-element.19), channel_id=1, source_target_pairs={{0,4},{4,0},{1,5},{5,1},{2,6},{6,2},{3,7},{7,3},{8,12},{12,8},{9,1... | collective-permute-start | bytes 393224 | tf_op jit(solution)/shard_map/ppermute | solution.py:701
  12.5 0.7 copy-start.5
  14.9 21.1 %all-to-all-start = ((f32[32,2,128]{2,1,0:T(2,128)}), f32[32,2,128]{2,1,0:T(2,128)S(1)}, u32[]{:S(2)}, u32[]{:S(2)}) async-start(f32[32,2,128]{2,1,0:T(2,128)} %bitcast.12), calls=%async_computation | async-start | bytes 65536 | tf_op jit(solution)/shard_map/all_to_all | solution.py:702
  23.3 23.3 %collective-permute-start = (f32[33,8,128]{2,1,0:T(8,128)S(1)}, f32[33,8,128]{2,1,0:T(8,128)S(1)}, u32[]{:S(2)}, u32[]{:S(2)}) collective-permute-start(f32[33,8,128]{2,1,0:T(8,128)S(1)} %get-tuple-element.18), channel_id=1, source_target_pairs={{0,4},{4,0},{1,5},{5,1},{2,6},{6,2},{3,7},{7,3},{8,12},{12,8},{9,1... | collective-permute-start | bytes 405512 | tf_op jit(solution)/shard_map/ppermute | solution.py:703
  33.3 13.3 %collective-permute-start.2 = (f32[32,8,128]{2,1,0:T(8,128)S(1)}, f32[32,8,128]{2,1,0:T(8,128)S(1)}, u32[]{:S(2)}, u32[]{:S(2)}) collective-permute-start(f32[32,8,128]{2,1,0:T(8,128)S(1)} %collective-permute-done.1), channel_id=1, source_target_pairs={{0,8},{8,16},{16,24},{12,4},{20,12},{28,20},{1,9},{9,17},{17,25},{... | collective-permute-start | bytes 393224 | tf_op jit(solution)/shard_map/ppermute | solution.py:707
  36.0 12.0 %collective-permute-start.3 = (f32[4,8,128]{2,1,0:T(8,128)S(1)}, f32[4,8,128]{2,1,0:T(8,128)S(1)}, u32[]{:S(2)}, u32[]{:S(2)}) collective-permute-start(f32[4,8,128]{2,1,0:T(8,128)S(1)} %bitcast.17), channel_id=1, source_target_pairs={{0,8},{8,16},{16,24},{12,4},{20,12},{28,20},{1,9},{9,17},{17,25},{... | collective-permute-start | bytes 49160 | tf_op jit(solution)/shard_map/ppermute | solution.py:708
  46.6 1.4 %copy-start.3 = (f32[27,4,8,128]{3,2,1,0:T(8,128)S(1)}, f32[27,4,8,128]{3,2,1,0:T(8,128)}, u32[]{:S(2)}) copy-start(f32[27,4,8,128]{3,2,1,0:T(8,128)} %pop.1) | copy-start | bytes 1327108
  47.3 24.0 %collective-permute-start.6 = (f32[70,8,128]{2,1,0:T(8,128)S(1)}, f32[70,8,128]{2,1,0:T(8,128)S(1)}, u32[]{:S(2)}, u32[]{:S(2)}) collective-permute-start(f32[70,8,128]{2,1,0:T(8,128)S(1)} %get-tuple-element.25.sw), channel_id=1, source_target_pairs={{0,480},{480,0},{1,481},{481,1},{2,482},{482,2},{3,483},{483,3},{4... | collective-permute-start | bytes 860168 | tf_op jit(solution)/shard_map/ppermute | solution.py:722
  50.5 14.7 %collective-permute-start.4 = (f32[69,8,128]{2,1,0:T(8,128)S(1)}, f32[69,8,128]{2,1,0:T(8,128)S(1)}, u32[]{:S(2)}, u32[]{:S(2)}) collective-permute-start(f32[69,8,128]{2,1,0:T(8,128)S(1)} %get-tuple-element.22), channel_id=1, source_target_pairs={{0,32},{32,0},{64,96},{96,64},{128,160},{160,128},{192,224},{224,1... | collective-permute-start | bytes 847880 | tf_op jit(solution)/shard_map/ppermute | solution.py:739
  63.3 7.9 %collective-permute-start.5 = (f32[69,8,128]{2,1,0:T(8,128)S(1)}, f32[69,8,128]{2,1,0:T(8,128)S(1)}, u32[]{:S(2)}, u32[]{:S(2)}) collective-permute-start(f32[69,8,128]{2,1,0:T(8,128)S(1)} %get-tuple-element.23), channel_id=1, source_target_pairs={{32,64},{96,128},{160,192},{224,256},{288,320},{352,384},{416,448}... | collective-permute-start | bytes 847880 | tf_op jit(solution)/shard_map/ppermute | solution.py:741
  73.3 5.8 %collective-permute-start.7 = (f32[8,8,128]{2,1,0:T(8,128)S(1)}, f32[8,8,128]{2,1,0:T(8,128)S(1)}, u32[]{:S(2)}, u32[]{:S(2)}) collective-permute-start(f32[8,8,128]{2,1,0:T(8,128)S(1)} %get-tuple-element.28), channel_id=1, source_target_pairs={{0,1},{1,0},{2,3},{3,2},{4,5},{5,4},{6,7},{7,6},{8,9},{9,8},{10,11... | collective-permute-start | bytes 98312 | tf_op jit(solution)/shard_map/ppermute | solution.py:756
  76.5 5.8 %collective-permute-start.8 = (f32[8,8,128]{2,1,0:T(8,128)S(1)}, f32[8,8,128]{2,1,0:T(8,128)S(1)}, u32[]{:S(2)}, u32[]{:S(2)}) collective-permute-start(f32[8,8,128]{2,1,0:T(8,128)S(1)} %get-tuple-element.29), channel_id=1, source_target_pairs={{1,2},{2,1},{5,6},{6,5},{9,10},{10,9},{13,14},{14,13},{17,18},{18,... | collective-permute-start | bytes 98312 | tf_op jit(solution)/shard_map/ppermute | solution.py:758

commit v2 on v1

--- a/solution.py
+++ b/solution.py
@@ -22,21 +22,19 @@
 UP = [moving(axis, 1) for axis in range(3)]
 DOWN = [moving(axis, -1) for axis in range(3)]
 
-T_DEEP, T_COARSE, T_FACE = 14, 23, 32
+T_DEEP, T_COARSE, T_LEVEL, T_FACE = 14, 23, 22, 33
 X_ROWS, X_COARSE, T_X = 40, 60, 69
 
 
-def level_rows(way):
-    rows = [(ch, 0) for ch in range(46)] + [(ch, 1) for ch in range(27)]
-    rows += [(27 + j, 1) for j in range(9) if stencil[UP[0][j]][1] == way]
-    rows += [(36 + j, 1) for j in range(9) if stencil[DOWN[0][j]][1] == way]
+def level_rows():
+    rows = [(ch, 0) for ch in range(46)] + [(ch, 1) for ch in range(45)]
     spots = [(22, r, 64 * half) for r in range(4, 8) for half in range(2)]
     spots += [(27, r, 64) for r in range(8)]
-    spots += [(t, r, 64 * half) for t in range(28, 32) for r in range(8) for half in range(2)]
+    spots += [(t, r, 64 * half) for t in range(28, 33) for r in range(8) for half in range(2)]
     return dict(zip(rows, spots))
 
 
-LEVEL = {1: level_rows(1), -1: level_rows(-1)}
+LEVEL = level_rows()
 T_SW = 18
 
 z_items = [(0, x, ch) for x in range(1, 7) for ch in range(31)]
@@ -167,17 +165,11 @@
 
 
 def pack_kernel(
-    sc, pop_in, cpop_in, mask, inflow,
-    far, near, vel, cc, r127, rs, pop, cpop, rc, mom, faces, sems,
+    sc, pop, cpop, mask, inflow, faces, vel, cc, r127, rs, rc, mom,
 ):
     h = sc[S_H]
-    copies = [pltpu.make_async_copy(pop_in, pop, sems.at[0]), pltpu.make_async_copy(cpop_in, cpop, sems.at[1])]
-    for c in copies:
-        c.start()
     rc[...] = jnp.zeros(rc.shape, jnp.float32)
     faces[...] = jnp.zeros(faces.shape, jnp.float32)
-    for c in copies:
-        c.wait()
     for x in range(4):
         density, m = moments([pop[i, x] for i in range(27)])
         inverse = 1.0 / (density + (1.0 - mask[x].astype(jnp.float32)))
@@ -226,7 +218,7 @@
             lane = 64 * (j // 5)
             for x in range(8):
                 faces[face, T_COARSE + j % 5, x : x + 1, lane : lane + 64] = cc[x, i, r : r + 1, 0:64]
-        for (ch, depth), (tile, at, lane) in LEVEL[way].items():
+        for (ch, depth), (tile, at, lane) in LEVEL.items():
             r = coarse_depths[depth]
             if ch < 27:
                 value = rc[ch, 7, r : r + 1, 0:64]
@@ -237,8 +229,6 @@
             else:
                 value = inflow[r : r + 1, :]
             faces[face, tile, at : at + 1, lane : lane + 64] = value
-    near[0:T_FACE] = faces[0]
-    far[...] = faces[1]
 
 
 def particle_fields(rows):
@@ -277,46 +267,11 @@
 
 def choose(sc, near, fwd):
     lower = sc[S_H] == 0
-    return (lambda t: jnp.where(lower, near[t], fwd[t])), (lambda t: jnp.where(lower, fwd[t], near[t]))
-
-
-def level_kernel(sc, cc, r127, rs, inflow, near, fwd, sw, inf, hi, lo):
-    up, down = choose(sc, near, fwd)
-    for t in range(22, T_FACE):
-        hi[t], lo[t] = up(t), down(t)
-    for t in range(T_SW):
-        sw[t] = jnp.zeros((8, 128), jnp.float32)
-    inf[...] = jnp.zeros((8, 128), jnp.float32)
-    inf[0:4, 0:64] = inflow[...]
-
-    def halo(ch, ref, to):
-        for face, way, rows in ((hi, -1, (4, 5)), (lo, 1, (7, 6))):
-            for depth in range(2):
-                spot = LEVEL[way].get((ch, depth))
-                if spot is not None:
-                    tile, at, lane = spot
-                    r = rows[depth]
-                    ref[r : r + 1, to : to + 64] = face[tile, at : at + 1, lane : lane + 64]
-
-    halo(45, inf, 0)
-
-    @pl.when(sc[S_FIRST] == 1)
-    def _():
-        for j in range(9):
-            to = 64 * (j % 2)
-            sw[j // 2, 0:4, to : to + 64] = rs[j, 0:4, 0:64]
-            halo(36 + j, sw.at[j // 2], to)
-
-    @pl.when(sc[S_FIRST] == 0)
-    def _():
-        for ch in range(36):
-            to = 64 * (ch % 2)
-            own = r127.at[ch] if ch < 27 else cc.at[6, UP[0][ch - 27]]
-            sw[ch // 2, 0:4, to : to + 64] = own[0:4, 0:64]
-            halo(ch, sw.at[ch // 2], to)
-
-
-def deposit_kernel(sc, pop, mask, vel, cc, near, fwd, arr, third_in, ye, xa, xb, ccy, hi, lo):
+    return (lambda t: jnp.where(lower, near[0, t], fwd[t])), (lambda t: jnp.where(lower, fwd[t], near[0, t]))
+
+
+def deposit_kernel(sc, pop, mask, vel, cc, near, fwd, arr, third_in, corner, ends, ye, xb, xa, ccy, hi, lo):
+    del corner, ends
     h = sc[S_H]
     lower = h == 0
     up, down = choose(sc, near, fwd)
@@ -427,7 +382,47 @@
     return (lambda t: jnp.where(even, a[t], b[t])), (lambda t: jnp.where(even, b[t], a[t]))
 
 
-def column_kernel(sc, ye, xar, xbr, swr, ccy, sw, inf, za, zb):
+def level_layers(sc, rs, inflow, near, fwd, ends, corner, swr, sw, inf):
+    wide = T_FACE - T_LEVEL
+    for h in range(2):
+        here, there, other, beyond = ((3, 2), (0, 1), (4, 5), (7, 6)) if h == 0 else ((0, 1), (3, 2), (7, 6), (4, 5))
+
+        def put(ch, source, base, rows, ref, to):
+            for depth in range(2):
+                if (ch, depth) in LEVEL:
+                    tile, at, lane = LEVEL[ch, depth]
+                    r = rows[depth]
+                    ref[r : r + 1, to : to + 64] = source[tile + base, at : at + 1, lane : lane + 64]
+
+        def received(channels):
+            for q, ch in enumerate(channels):
+                ref, to = swr.at[q // 2], 64 * (q % 2)
+                put(ch, ends, -T_LEVEL, here, ref, to)
+                put(ch, ends, wide - T_LEVEL, there, ref, to)
+                put(ch, ends, 2 * wide - T_LEVEL, other, ref, to)
+                put(ch, corner, -T_LEVEL, beyond, ref, to)
+
+        @pl.when((sc[S_FIRST] == 1) & (sc[S_H] == h))
+        def _():
+            received(range(36))
+            for j in range(9):
+                ref, to = sw.at[j // 2], 64 * (j % 2)
+                ref[0:4, to : to + 64] = rs[j, 0:4, 0:64]
+                put(36 + j, near.at[0], 0, other, ref, to)
+                put(36 + j, fwd, 0, beyond, ref, to)
+            inf[0:4, 0:64] = inflow[...]
+            put(45, near.at[0], 0, other, inf, 0)
+            put(45, fwd, 0, beyond, inf, 0)
+
+        @pl.when((sc[S_LAST] == 1) & (sc[S_H] == h))
+        def _():
+            received(range(36, 45))
+
+
+def column_kernel(
+    sc, ye, xbr, xar, ccy, rs, inflow, near, fwd, ends, corner, za, zb, swr, sw, inf
+):
+    level_layers(sc, rs, inflow, near, fwd, ends, corner, swr, sw, inf)
     up, down = pick(sc, S_CORE, xar, xbr)
     lane = iota((16, 128), 1)
     lane8 = iota((8, 128), 1)
@@ -468,7 +463,7 @@
 
 
 def step_kernel(
-    sc, ye, xar, xbr, swr, ccy, sw, inf, zar, zbr, fine, coarse, p1, p2, gx, fx, ce, gr, late
+    sc, ye, xbr, xar, swr, ccy, sw, inf, zar, zbr, fine, coarse, p1, p2, gx, fx, ce, gr, late
 ):
     up, down = pick(sc, S_CORE, xar, xbr)
     zup, zdown = pick(sc, S_ODD, zar, zbr)
@@ -664,25 +659,22 @@
             (gz < n_gz - 1).astype(jnp.int32),
         ]
     ).astype(jnp.int32)
-    far, near, vel, cc, r127, rs = call(
+    faces, vel, cc, r127, rs = call(
         pack_kernel,
         "pack",
         [
-            f32(T_FACE, 8, 128),
-            f32(T_FACE + 1, 8, 128),
+            f32(2, T_FACE, 8, 128),
             f32(3, 4, 8, 128),
             f32(8, 27, 8, 128),
             f32(27, 8, 128),
             f32(9, 8, 128),
         ],
-        [(27, 4, 8, 128), (27, 8, 4, 64), (27, 8, 8, 128), (4, 4, 8, 128), (2, T_FACE, 8, 128)],
+        [(27, 8, 8, 128), (4, 4, 8, 128)],
         sc,
         pop,
         cpop,
         mask,
         inflow,
-        held=2,
-        cost=1_000_000_000,
     )
     (outbox,) = call(
         route_kernel,
@@ -698,29 +690,29 @@
         rs,
         cost=50_000_000_000,
     )
-    far = lax.ppermute(far, "h", [(0, 1), (1, 0)])
+    last = n_gx - 1
+    spot = lambda x, y, z: (x * n_y + y) * 2 + z
+    far_ends = [(spot(a, y, 1), spot(b, y + 1, 0)) for a, b in ((0, last), (last, 0)) for y in range(n_y - 1)]
+    corner = lax.ppermute(
+        faces[1, T_LEVEL:T_FACE], ("gx", "y", "h"), far_ends + [(j, i) for i, j in far_ends]
+    )
+    near = lax.ppermute(faces, "h", [(0, 1), (1, 0)])
     arr = lax.all_to_all(outbox.reshape(2 * n_gx, 2, 128), ("gx", "h"), 0, 0, tiled=True)
-    near = lax.ppermute(near, "h", [(0, 1), (1, 0)])
+    near_ends = [(2 * last + 1, 0), (2 * last, 1)]
+    ends = lax.ppermute(
+        jnp.concatenate(
+            [near[0, T_LEVEL:T_FACE], near[1, T_LEVEL:T_FACE], faces[0, T_LEVEL:T_FACE]], axis=0
+        ),
+        ("gx", "h"),
+        near_ends + [(j, i) for i, j in near_ends],
+    )
     onward = [(2 * y, 2 * y + 2) for y in range(n_y - 1)]
     onward += [(2 * y + 3, 2 * y + 1) for y in range(n_y - 1)]
     partner = jnp.where(h == 0, arr[1::2], arr[0::2]).reshape(4, 8, 128)
-    fwd = lax.ppermute(far, ("y", "h"), onward)
+    fwd = lax.ppermute(near[1], ("y", "h"), onward)
+    partner, _ = lax.optimization_barrier((partner, near))
     third = lax.ppermute(partner, ("y", "h"), onward)
-    sw, inf = call(
-        level_kernel,
-        "level",
-        [f32(T_X + 1, 8, 128), f32(8, 128)],
-        [(T_FACE, 8, 128), (T_FACE, 8, 128)],
-        sc,
-        cc,
-        r127,
-        rs,
-        inflow,
-        near,
-        fwd,
-    )
-    swr = lax.ppermute(sw, "gx", [(0, n_gx - 1), (n_gx - 1, 0)])
-    ye, xa, xb, ccy = call(
+    ye, xb, xa, ccy = call(
         deposit_kernel,
         "deposit",
         [f32(4, 31, 16, 128), f32(T_X, 8, 128), f32(T_X, 8, 128), f32(8, 27, 8, 128)],
@@ -734,24 +726,29 @@
         fwd,
         arr,
         third,
+        corner,
+        ends,
         cost=50_000_000_000,
     )
-    xar = lax.ppermute(xa, "gx", [(i, i ^ 1) for i in range(n_gx)])
     inner = [(i, i + 1) for i in range(1, n_gx - 1, 2)]
     xbr = lax.ppermute(xb, "gx", inner + [(j, i) for i, j in inner])
-    za, zb = call(
+    xar = lax.ppermute(xa, "gx", [(i, i ^ 1) for i in range(n_gx)])
+    za, zb, swr, sw, inf = call(
         column_kernel,
         "columns",
-        [f32(8, 8, 128), f32(8, 8, 128)],
+        [f32(8, 8, 128), f32(8, 8, 128), f32(T_SW, 8, 128), f32(5, 8, 128), f32(8, 128)],
         [],
         sc,
         ye,
+        xbr,
         xar,
-        xbr,
-        swr,
         ccy,
-        sw,
-        inf,
+        rs,
+        inflow,
+        near,
+        fwd,
+        ends,
+        corner,
     )
     zar = lax.ppermute(za, "gz", [(i, i ^ 1) for i in range(n_gz)])
     inner = [(i, i + 1) for i in range(1, n_gz - 1, 2)]
@@ -771,8 +768,8 @@
         ],
         sc,
         ye,
+        xbr,
         xar,
-        xbr,
         swr,
         ccy,
         sw,

time: 88.3 us -> 84.3 us (0.955)
  the two profiles are of different devices: /device:TPU:508 before, /device:TPU:12 now
where the time goes in v2:
time: 84.3 us; the launch traced here: 83.8 us
  starting transfers between devices  52.5 us (62%)
  Pallas kernels  16.5 us (20%)
  waiting for transfers between devices  10.4 us (12%)
  local copies, waits for them, and re-layouts  3.45 us (4%)
  between operations  0.92 us (1%)
    pallas_call x5, Pallas kernels, call(): pl.pallas_call(kernel, out_shape=out_shape, in_specs=[pl.BlockSpec(memory...  16.5 us
    ppermute x1, starting transfers between devices, body(): near = lax.ppermute(faces, 'h', [(0, 1), (1, 0)])  15.8 us
    ppermute x1, starting transfers between devices, body(): lax.ppermute(jnp.concatenate([near[0, T_LEVEL:T_FACE], near[1, T_LEVEL:T_...  11.6 us
    all_to_all x1, starting transfers between devices, body(): lax.all_to_all(outbox.reshape(2 * n_gx, 2, 128), ('gx', 'h'), 0, 0, tiled...  5.41 us
    ppermute x1, starting transfers between devices, body(): lax.ppermute(faces[1, T_LEVEL:T_FACE], ('gx', 'y', 'h'), far_ends + [(j,...  4.76 us
    ppermute x1, starting transfers between devices, body(): fwd = lax.ppermute(near[1], ('y', 'h'), onward)  3.48 us
    ppermute x1, starting transfers between devices, body(): third = lax.ppermute(partner, ('y', 'h'), onward)  3.48 us
    unnamed x22, local copies, waits for them, and re-layouts  3.33 us
  transfers between devices with their start and end apart: 10, of which 5 were waited for; matrix products, arithmetic and copies ran while one was open for 0% of the time, Pallas kernels for 2%

profile of v2, /device:TPU:12, one launch (start us, length us, event | category | flops | bytes accessed | tf_op | source)
XLA Modules:
  0.0 83.8 jit_solution(12033118912837085466)
XLA Ops:
  0.7 0.1 stack.63.sc
  0.8 0.6 copy-done.3
  1.4 1.0 %copy-done = f32[27,8,4,64]{3,2,1,0:T(4,128)S(1)} copy-done((f32[27,8,4,64]{3,2,1,0:T(4,128)S(1)}, f32[27,8,4,64]{3,2,1,0:T(4,128)}, u32[]{:S(2)}) %copy-start) | copy-done | bytes 221208
  2.4 1.0 %copy-done.1 = f32[27,4,8,128]{3,2,1,0:T(8,128)S(1)} copy-done((f32[27,4,8,128]{3,2,1,0:T(8,128)S(1)}, f32[27,4,8,128]{3,2,1,0:T(8,128)}, u32[]{:S(2)}) %copy-start.1) | copy-done | bytes 442392
  3.4 2.6 %pack.1 = (f32[2,33,8,128]{3,2,1,0:T(8,128)S(1)}, f32[3,4,8,128]{3,2,1,0:T(8,128)S(1)}, f32[8,27,8,128]{3,2,1,0:T(8,128)S(1)}, f32[27,8,128]{2,1,0:T(8,128)}, f32[9,8,128]{2,1,0:T(8,128)S(1)}) custom-call(s32[9]{0:T(128)S(1)} %stack.63.sc, f32[27,4,8,128]{3,2,1,0:T(8,128)S(1)} %copy-done.1, f32[27,8,4,64]{3,2,1,0:T(4,128)S(1)} %copy-done, ...), custom_call_target="tpu_custom_call" | custom-call | tf_op jit(solution)/shard_map/pack/pallas_call | solution.py:632
  6.0 15.8 %collective-permute-start = (f32[2,33,8,128]{3,2,1,0:T(8,128)S(1)}, f32[2,33,8,128]{3,2,1,0:T(8,128)S(1)}, u32[]{:S(2)}, u32[]{:S(2)}) collective-permute-start(f32[2,33,8,128]{3,2,1,0:T(8,128)S(1)} %get-tuple-element.18), channel_id=1, source_target_pairs={{0,4},{4,0},{1,5},{5,1},{2,6},{6,2},{3,7},{7,3},{8,12},{12,8},{9,1... | collective-permute-start | bytes 811016 | tf_op jit(solution)/shard_map/ppermute | solution.py:699
  21.9 0.0 copy-start.6
  21.9 0.0 copy-start.7
  21.9 0.0 copy-start.5
  21.9 0.6 copy-done.6
  22.6 0.0 copy-done.7
  22.6 0.0 copy-done.5
  22.6 1.8 %route.1 = f32[64,128]{1,0:T(8,128)} custom-call(s32[9]{0:T(128)S(1)} %stack.63.sc, s32[1,256]{1,0:T(1,128)S(1)} %bitcast.24, s32[1,256]{1,0:T(1,128)S(1)} %bitcast.25, f32[1,1,1,3,256]{4,3,2,1,0:T(4,128)S(1)} %copy.11.pvel, f32[1,1,1,3,256]{4,3,2,1,0:T(4,128)S(1)} %copy.12.pfrac, f32[1,256]{1,0:T(1,128)S(1)} %bitcast.26, ...), custom_call_target="tpu_custom_call" | custom-call | flops 49999998976 | bytes 1 | tf_op jit(solution)/shard_map/route/pallas_call | solution.py:632
  24.3 5.4 %all-to-all-start = ((f32[32,2,128]{2,1,0:T(2,128)}), f32[32,2,128]{2,1,0:T(2,128)S(1)}, u32[]{:S(2)}, u32[]{:S(2)}) async-start(f32[32,2,128]{2,1,0:T(2,128)} %bitcast.13), calls=%async_computation | async-start | bytes 65536 | tf_op jit(solution)/shard_map/all_to_all | solution.py:700
  29.8 0.0 copy-start.2
  29.8 4.8 %collective-permute-start.3 = (f32[11,8,128]{2,1,0:T(8,128)S(1)}, f32[11,8,128]{2,1,0:T(8,128)S(1)}, u32[]{:S(2)}, u32[]{:S(2)}) collective-permute-start(f32[11,8,128]{2,1,0:T(8,128)S(1)} %get-tuple-element.33), channel_id=1, source_target_pairs={{4,488},{12,496},{20,504},{484,8},{492,16},{500,24},{488,4},{496,1... | collective-permute-start | bytes 135176 | tf_op jit(solution)/shard_map/ppermute | solution.py:696
  34.6 3.5 %collective-permute-start.1 = (f32[33,8,128]{2,1,0:T(8,128)S(1)}, f32[33,8,128]{2,1,0:T(8,128)S(1)}, u32[]{:S(2)}, u32[]{:S(2)}) collective-permute-start(f32[33,8,128]{2,1,0:T(8,128)S(1)} %slice_bitcast_fusion), channel_id=1, source_target_pairs={{0,8},{8,16},{16,24},{12,4},{20,12},{28,20},{1,9},{9,17},{17,25},{... | collective-permute-start | bytes 405512 | tf_op jit(solution)/shard_map/ppermute | solution.py:712
  38.1 11.6 %collective-permute-start.4 = (f32[33,8,128]{2,1,0:T(8,128)S(1)}, f32[33,8,128]{2,1,0:T(8,128)S(1)}, u32[]{:S(2)}, u32[]{:S(2)}) collective-permute-start(f32[33,8,128]{2,1,0:T(8,128)S(1)} %pad_maximum_fusion), channel_id=1, source_target_pairs={{484,0},{480,4},{0,484},{4,480},{485,1},{481,5},{1,485},{5,481},{4... | collective-permute-start | bytes 405512 | tf_op jit(solution)/shard_map/ppermute | solution.py:702
  49.7 3.2 %all-to-all-done.arr = f32[32,2,128]{2,1,0:T(2,128)S(1)} async-done(((f32[32,2,128]{2,1,0:T(2,128)}), f32[32,2,128]{2,1,0:T(2,128)S(1)}, u32[]{:S(2)}, u32[]{:S(2)}) %all-to-all-start) | async-done | bytes 32800 | tf_op jit(solution)/shard_map/all_to_all | solution.py:700
  52.9 3.5 %collective-permute-start.2 = (f32[4,8,128]{2,1,0:T(8,128)S(1)}, f32[4,8,128]{2,1,0:T(8,128)S(1)}, u32[]{:S(2)}, u32[]{:S(2)}) collective-permute-start(f32[4,8,128]{2,1,0:T(8,128)S(1)} %bitcast.27), channel_id=1, source_target_pairs={{0,8},{8,16},{16,24},{12,4},{20,12},{28,20},{1,9},{9,17},{17,25},{... | collective-permute-start | bytes 49160 | tf_op jit(solution)/shard_map/ppermute | solution.py:714
  56.4 2.1 %collective-permute-done.2.third_in = f32[4,8,128]{2,1,0:T(8,128)S(1)} collective-permute-done((f32[4,8,128]{2,1,0:T(8,128)S(1)}, f32[4,8,128]{2,1,0:T(8,128)S(1)}, u32[]{:S(2)}, u32[]{:S(2)}) %collective-permute-start.2) | collective-permute-done | bytes 16416 | tf_op jit(solution)/shard_map/ppermute | solution.py:714
  58.6 0.0 collective-permute-done.1.fwd
  58.6 2.5 %deposit.1 = (f32[4,31,16,128]{3,2,1,0:T(8,128)S(1)}, f32[69,8,128]{2,1,0:T(8,128)S(1)}, f32[69,8,128]{2,1,0:T(8,128)S(1)}, f32[8,27,8,128]{3,2,1,0:T(8,128)S(1)}) custom-call(s32[9]{0:T(128)S(1)} %stack.63.sc, f32[27,4,8,128]{3,2,1,0:T(8,128)S(1)} %copy-done.2, s32[4,8,128]{2,1,0:T(8,128)S(1)} %copy-done.3, f32[3,4,8,128]{3,2,1,0:T(8,128)S(1)} %get-tuple-element.16.vel, ...), custom_call_target="tpu_custom_call" | custom-call | flops 49999998976 | bytes 1 | tf_op jit(solution)/shard_map/deposit/pallas_call | solution.py:632
  61.1 0.7 collective-permute-start.5
  61.8 2.2 %collective-permute-start.6 = (f32[69,8,128]{2,1,0:T(8,128)S(1)}, f32[69,8,128]{2,1,0:T(8,128)S(1)}, u32[]{:S(2)}, u32[]{:S(2)}) collective-permute-start(f32[69,8,128]{2,1,0:T(8,128)S(1)} %get-tuple-element.23), channel_id=1, source_target_pairs={{0,32},{32,0},{64,96},{96,64},{128,160},{160,128},{192,224},{224,1... | collective-permute-start | bytes 847880 | tf_op jit(solution)/shard_map/ppermute | solution.py:735
  64.1 1.2 %collective-permute-done.6.xar = f32[69,8,128]{2,1,0:T(8,128)S(1)} collective-permute-done((f32[69,8,128]{2,1,0:T(8,128)S(1)}, f32[69,8,128]{2,1,0:T(8,128)S(1)}, u32[]{:S(2)}, u32[]{:S(2)}) %collective-permute-start.6) | collective-permute-done | bytes 282656 | tf_op jit(solution)/shard_map/ppermute | solution.py:735
  65.3 2.2 %columns.1 = (f32[8,8,128]{2,1,0:T(8,128)S(1)}, f32[8,8,128]{2,1,0:T(8,128)S(1)}, f32[18,8,128]{2,1,0:T(8,128)S(1)}, f32[5,8,128]{2,1,0:T(8,128)S(1)}, f32[8,128]{1,0:T(8,128)S(1)}) custom-call(s32[9]{0:T(128)S(1)} %stack.63.sc, f32[4,31,16,128]{3,2,1,0:T(8,128)S(1)} %get-tuple-element.21.ye, f32[69,8,128]{2,1,0:T(8,128)S(1)} %collective-permute-done.5.xbr, ...), custom_call_target="tpu_custom_call" | custom-call | tf_op jit(solution)/shard_map/columns/pallas_call | solution.py:632
  67.5 3.1 %collective-permute-start.7 = (f32[8,8,128]{2,1,0:T(8,128)S(1)}, f32[8,8,128]{2,1,0:T(8,128)S(1)}, u32[]{:S(2)}, u32[]{:S(2)}) collective-permute-start(f32[8,8,128]{2,1,0:T(8,128)S(1)} %get-tuple-element.28), channel_id=1, source_target_pairs={{0,1},{1,0},{2,3},{3,2},{4,5},{5,4},{6,7},{7,6},{8,9},{9,8},{10,11... | collective-permute-start | bytes 98312 | tf_op jit(solution)/shard_map/ppermute | solution.py:753
  70.6 1.9 %collective-permute-start.8 = (f32[8,8,128]{2,1,0:T(8,128)S(1)}, f32[8,8,128]{2,1,0:T(8,128)S(1)}, u32[]{:S(2)}, u32[]{:S(2)}) collective-permute-start(f32[8,8,128]{2,1,0:T(8,128)S(1)} %get-tuple-element.29), channel_id=1, source_target_pairs={{1,2},{2,1},{5,6},{6,5},{9,10},{10,9},{13,14},{14,13},{17,18},{18,... | collective-permute-start | bytes 98312 | tf_op jit(solution)/shard_map/ppermute | solution.py:755
  72.6 0.8 collective-permute-done.7.zar
  73.3 3.1 %collective-permute-done.8.zbr = f32[8,8,128]{2,1,0:T(8,128)S(1)} collective-permute-done((f32[8,8,128]{2,1,0:T(8,128)S(1)}, f32[8,8,128]{2,1,0:T(8,128)S(1)}, u32[]{:S(2)}, u32[]{:S(2)}) %collective-permute-start.8) | collective-permute-done | bytes 32800 | tf_op jit(solution)/shard_map/ppermute | solution.py:755
  76.5 7.3 %steps.1 = (f32[27,4,8,128]{3,2,1,0:T(8,128)}, f32[27,8,4,64]{3,2,1,0:T(4,128)}) custom-call(s32[9]{0:T(128)S(1)} %stack.63.sc, f32[4,31,16,128]{3,2,1,0:T(8,128)S(1)} %get-tuple-element.21.ye, f32[69,8,128]{2,1,0:T(8,128)S(1)} %collective-permute-done.5.xbr, f32[69,8,128]{2,1,0:T(8,128)S(1)} %collective-permute-done.6.xar, ...), custom_call_target="tpu_custom_call" | custom-call | tf_op jit(solution)/shard_map/steps/pallas_call | solution.py:632
  (21 shorter events, 0.1 us)
Async XLA Ops:
  0.7 0.7 copy-start.3
  0.7 0.7 copy-start.4
  1.4 1.0 %copy-start = (f32[27,8,4,64]{3,2,1,0:T(4,128)S(1)}, f32[27,8,4,64]{3,2,1,0:T(4,128)}, u32[]{:S(2)}) copy-start(f32[27,8,4,64]{3,2,1,0:T(4,128)} %cpop.1) | copy-start | bytes 663556
  2.4 1.0 %copy-start.1 = (f32[27,4,8,128]{3,2,1,0:T(8,128)S(1)}, f32[27,4,8,128]{3,2,1,0:T(8,128)}, u32[]{:S(2)}) copy-start(f32[27,4,8,128]{3,2,1,0:T(8,128)} %pop.3) | copy-start | bytes 1327108
  3.4 18.4 %copy-start.8 = (f32[1,1,1,3,256]{4,2,3,1,0:T(1,128)S(1)}, f32[1,1,1,3,256]{4,2,3,1,0:T(1,128)}, u32[]{:S(2)}) copy-start(f32[1,1,1,3,256]{4,2,3,1,0:T(1,128)} %param.15) | copy-start | bytes 9220
  6.0 15.9 %copy-start.9 = (f32[1,1,1,3,256]{4,2,3,1,0:T(1,128)S(1)}, f32[1,1,1,3,256]{4,2,3,1,0:T(1,128)}, u32[]{:S(2)}) copy-start(f32[1,1,1,3,256]{4,2,3,1,0:T(1,128)} %param.16) | copy-start | bytes 9220
  6.0 28.6 %collective-permute-start = (f32[2,33,8,128]{3,2,1,0:T(8,128)S(1)}, f32[2,33,8,128]{3,2,1,0:T(8,128)S(1)}, u32[]{:S(2)}, u32[]{:S(2)}) collective-permute-start(f32[2,33,8,128]{3,2,1,0:T(8,128)S(1)} %get-tuple-element.18), channel_id=1, source_target_pairs={{0,4},{4,0},{1,5},{5,1},{2,6},{6,2},{3,7},{7,3},{8,12},{12,8},{9,1... | collective-permute-start | bytes 811016 | tf_op jit(solution)/shard_map/ppermute | solution.py:699
  21.9 0.7 copy-start.6
  21.9 0.7 copy-start.7
  21.9 0.7 copy-start.5
  24.3 28.6 %all-to-all-start = ((f32[32,2,128]{2,1,0:T(2,128)}), f32[32,2,128]{2,1,0:T(2,128)S(1)}, u32[]{:S(2)}, u32[]{:S(2)}) async-start(f32[32,2,128]{2,1,0:T(2,128)} %bitcast.13), calls=%async_computation | async-start | bytes 65536 | tf_op jit(solution)/shard_map/all_to_all | solution.py:700
  29.8 28.8 %copy-start.2 = (f32[27,4,8,128]{3,2,1,0:T(8,128)S(1)}, f32[27,4,8,128]{3,2,1,0:T(8,128)}, u32[]{:S(2)}) copy-start(f32[27,4,8,128]{3,2,1,0:T(8,128)} %pop.3) | copy-start | bytes 1327108
  29.8 26.6 %collective-permute-start.3 = (f32[11,8,128]{2,1,0:T(8,128)S(1)}, f32[11,8,128]{2,1,0:T(8,128)S(1)}, u32[]{:S(2)}, u32[]{:S(2)}) collective-permute-start(f32[11,8,128]{2,1,0:T(8,128)S(1)} %get-tuple-element.33), channel_id=1, source_target_pairs={{4,488},{12,496},{20,504},{484,8},{492,16},{500,24},{488,4},{496,1... | collective-permute-start | bytes 135176 | tf_op jit(solution)/shard_map/ppermute | solution.py:696
  34.6 24.0 %collective-permute-start.1 = (f32[33,8,128]{2,1,0:T(8,128)S(1)}, f32[33,8,128]{2,1,0:T(8,128)S(1)}, u32[]{:S(2)}, u32[]{:S(2)}) collective-permute-start(f32[33,8,128]{2,1,0:T(8,128)S(1)} %slice_bitcast_fusion), channel_id=1, source_target_pairs={{0,8},{8,16},{16,24},{12,4},{20,12},{28,20},{1,9},{9,17},{17,25},{... | collective-permute-start | bytes 405512 | tf_op jit(solution)/shard_map/ppermute | solution.py:712
  38.1 20.5 %collective-permute-start.4 = (f32[33,8,128]{2,1,0:T(8,128)S(1)}, f32[33,8,128]{2,1,0:T(8,128)S(1)}, u32[]{:S(2)}, u32[]{:S(2)}) collective-permute-start(f32[33,8,128]{2,1,0:T(8,128)S(1)} %pad_maximum_fusion), channel_id=1, source_target_pairs={{484,0},{480,4},{0,484},{4,480},{485,1},{481,5},{1,485},{5,481},{4... | collective-permute-start | bytes 405512 | tf_op jit(solution)/shard_map/ppermute | solution.py:702
  52.9 5.6 %collective-permute-start.2 = (f32[4,8,128]{2,1,0:T(8,128)S(1)}, f32[4,8,128]{2,1,0:T(8,128)S(1)}, u32[]{:S(2)}, u32[]{:S(2)}) collective-permute-start(f32[4,8,128]{2,1,0:T(8,128)S(1)} %bitcast.27), channel_id=1, source_target_pairs={{0,8},{8,16},{16,24},{12,4},{20,12},{28,20},{1,9},{9,17},{17,25},{... | collective-permute-start | bytes 49160 | tf_op jit(solution)/shard_map/ppermute | solution.py:714
  61.1 2.9 %collective-permute-start.5 = (f32[69,8,128]{2,1,0:T(8,128)S(1)}, f32[69,8,128]{2,1,0:T(8,128)S(1)}, u32[]{:S(2)}, u32[]{:S(2)}) collective-permute-start(f32[69,8,128]{2,1,0:T(8,128)S(1)} %get-tuple-element.22), channel_id=1, source_target_pairs={{32,64},{96,128},{160,192},{224,256},{288,320},{352,384},{416,448}... | collective-permute-start | bytes 847880 | tf_op jit(solution)/shard_map/ppermute | solution.py:734
  61.8 3.5 %collective-permute-start.6 = (f32[69,8,128]{2,1,0:T(8,128)S(1)}, f32[69,8,128]{2,1,0:T(8,128)S(1)}, u32[]{:S(2)}, u32[]{:S(2)}) collective-permute-start(f32[69,8,128]{2,1,0:T(8,128)S(1)} %get-tuple-element.23), channel_id=1, source_target_pairs={{0,32},{32,0},{64,96},{96,64},{128,160},{160,128},{192,224},{224,1... | collective-permute-start | bytes 847880 | tf_op jit(solution)/shard_map/ppermute | solution.py:735
  67.5 5.8 %collective-permute-start.7 = (f32[8,8,128]{2,1,0:T(8,128)S(1)}, f32[8,8,128]{2,1,0:T(8,128)S(1)}, u32[]{:S(2)}, u32[]{:S(2)}) collective-permute-start(f32[8,8,128]{2,1,0:T(8,128)S(1)} %get-tuple-element.28), channel_id=1, source_target_pairs={{0,1},{1,0},{2,3},{3,2},{4,5},{5,4},{6,7},{7,6},{8,9},{9,8},{10,11... | collective-permute-start | bytes 98312 | tf_op jit(solution)/shard_map/ppermute | solution.py:753
  70.6 5.8 %collective-permute-start.8 = (f32[8,8,128]{2,1,0:T(8,128)S(1)}, f32[8,8,128]{2,1,0:T(8,128)S(1)}, u32[]{:S(2)}, u32[]{:S(2)}) collective-permute-start(f32[8,8,128]{2,1,0:T(8,128)S(1)} %get-tuple-element.29), channel_id=1, source_target_pairs={{1,2},{2,1},{5,6},{6,5},{9,10},{10,9},{13,14},{14,13},{17,18},{18,... | collective-permute-start | bytes 98312 | tf_op jit(solution)/shard_map/ppermute | solution.py:755

commit v3 on v2

--- a/solution.py
+++ b/solution.py
@@ -83,6 +83,18 @@
         precision=lax.Precision.HIGHEST,
         preferred_element_type=jnp.float32,
     )
+
+
+def select(value, pick, left=False):
+    total = None
+    pick = pick.astype(jnp.bfloat16)
+    for _ in range(3):
+        part = value.astype(jnp.bfloat16)
+        value = value - part.astype(jnp.float32)
+        a, b = (pick, part) if left else (part, pick)
+        product = jnp.dot(a, b, preferred_element_type=jnp.float32)
+        total = product if total is None else total + product
+    return total
 
 
 def moments(n):
@@ -188,7 +200,7 @@
     narrow = ((iota((128, 128), 0) >> 1) == iota((128, 128), 1)).astype(jnp.float32)
     down, across = iota((216, 216), 0), iota((216, 216), 1)
     low = ((down >> 3) == (across >> 3)) & (((across & 7) >> 1) == (down & 7))
-    mean = 0.125 * dot(low.astype(jnp.float32), dot(pair, narrow))
+    mean = 0.125 * select(select(pair, narrow), low.astype(jnp.float32), left=True)
     settled = interface([mean[8 * i : 8 * i + 8] for i in range(27)], restrict_factor)
     for j in range(9):
         rs[j] = settled[DOWN[0][j]]
@@ -564,7 +576,7 @@
         )
         for layer, to in ((n127, p1.at[1]), (later, late)):
             layer = interface(layer, prolong_factor)
-            fines = dot(tall, dot(jnp.concatenate(layer, axis=0), wide))
+            fines = select(select(jnp.concatenate(layer, axis=0), wide), tall, left=True)
             for i in range(27):
                 to[i] = jnp.where(within, fines[16 * i : 16 * i + 16], wall)
 

time: 84.3 us -> 83 us (0.985)
  the two profiles are of different devices: /device:TPU:12 before, /device:TPU:28 now
where the time goes in v3:
time: 83 us; the launch traced here: 82.5 us
  starting transfers between devices  50.3 us (61%)
  Pallas kernels  15.2 us (18%)
  waiting for transfers between devices  12.6 us (15%)
  local copies, waits for them, and re-layouts  3.45 us (4%)
  between operations  0.92 us (1%)
    ppermute x1, starting transfers between devices, body(): near = lax.ppermute(faces, 'h', [(0, 1), (1, 0)])  15.8 us
    pallas_call x5, Pallas kernels, call(): pl.pallas_call(kernel, out_shape=out_shape, in_specs=[pl.BlockSpec(memory...  15.2 us
    ppermute x1, starting transfers between devices, body(): lax.ppermute(jnp.concatenate([near[0, T_LEVEL:T_FACE], near[1, T_LEVEL:T_...  13.8 us
    all_to_all x1, starting transfers between devices, body(): lax.all_to_all(outbox.reshape(2 * n_gx, 2, 128), ('gx', 'h'), 0, 0, tiled...  5.41 us
    ppermute x1, starting transfers between devices, body(): lax.ppermute(faces[1, T_LEVEL:T_FACE], ('gx', 'y', 'h'), far_ends + [(j,...  5.05 us
    ppermute x1, waiting for transfers between devices, body(): third = lax.ppermute(partner, ('y', 'h'), onward)  4.32 us
    unnamed x22, local copies, waits for them, and re-layouts  3.33 us
    ppermute x1, waiting for transfers between devices, body(): zbr = lax.ppermute(zb, 'gz', inner + [(j, i) for i, j in inner])  3.12 us
  transfers between devices with their start and end apart: 10, of which 5 were waited for; matrix products, arithmetic and copies ran while one was open for 0% of the time, Pallas kernels for 2%

profile of v3, /device:TPU:28, one launch (start us, length us, event | category | flops | bytes accessed | tf_op | source)
XLA Modules:
  0.0 82.5 jit_solution(2324824647485385897)
XLA Ops:
  0.7 0.1 stack.63.sc
  0.8 0.6 copy-done.3
  1.4 1.0 %copy-done = f32[27,8,4,64]{3,2,1,0:T(4,128)S(1)} copy-done((f32[27,8,4,64]{3,2,1,0:T(4,128)S(1)}, f32[27,8,4,64]{3,2,1,0:T(4,128)}, u32[]{:S(2)}) %copy-start) | copy-done | bytes 221208
  2.4 1.0 %copy-done.1 = f32[27,4,8,128]{3,2,1,0:T(8,128)S(1)} copy-done((f32[27,4,8,128]{3,2,1,0:T(8,128)S(1)}, f32[27,4,8,128]{3,2,1,0:T(8,128)}, u32[]{:S(2)}) %copy-start.1) | copy-done | bytes 442392
  3.4 2.1 %pack.1 = (f32[2,33,8,128]{3,2,1,0:T(8,128)S(1)}, f32[3,4,8,128]{3,2,1,0:T(8,128)S(1)}, f32[8,27,8,128]{3,2,1,0:T(8,128)S(1)}, f32[27,8,128]{2,1,0:T(8,128)}, f32[9,8,128]{2,1,0:T(8,128)S(1)}) custom-call(s32[9]{0:T(128)S(1)} %stack.63.sc, f32[27,4,8,128]{3,2,1,0:T(8,128)S(1)} %copy-done.1, f32[27,8,4,64]{3,2,1,0:T(4,128)S(1)} %copy-done, ...), custom_call_target="tpu_custom_call" | custom-call | tf_op jit(solution)/shard_map/pack/pallas_call | solution.py:644
  5.5 15.8 %collective-permute-start = (f32[2,33,8,128]{3,2,1,0:T(8,128)S(1)}, f32[2,33,8,128]{3,2,1,0:T(8,128)S(1)}, u32[]{:S(2)}, u32[]{:S(2)}) collective-permute-start(f32[2,33,8,128]{3,2,1,0:T(8,128)S(1)} %get-tuple-element.18), channel_id=1, source_target_pairs={{0,4},{4,0},{1,5},{5,1},{2,6},{6,2},{3,7},{7,3},{8,12},{12,8},{9,1... | collective-permute-start | bytes 811016 | tf_op jit(solution)/shard_map/ppermute | solution.py:711
  21.4 0.0 copy-start.6
  21.4 0.0 copy-start.7
  21.4 0.0 copy-start.5
  21.4 0.6 copy-done.6
  22.1 0.0 copy-done.7
  22.1 0.0 copy-done.5
  22.1 1.8 %route.1 = f32[64,128]{1,0:T(8,128)} custom-call(s32[9]{0:T(128)S(1)} %stack.63.sc, s32[1,256]{1,0:T(1,128)S(1)} %bitcast.24, s32[1,256]{1,0:T(1,128)S(1)} %bitcast.25, f32[1,1,1,3,256]{4,3,2,1,0:T(4,128)S(1)} %copy.11.pvel, f32[1,1,1,3,256]{4,3,2,1,0:T(4,128)S(1)} %copy.12.pfrac, f32[1,256]{1,0:T(1,128)S(1)} %bitcast.26, ...), custom_call_target="tpu_custom_call" | custom-call | flops 49999998976 | bytes 1 | tf_op jit(solution)/shard_map/route/pallas_call | solution.py:644
  23.8 5.4 %all-to-all-start = ((f32[32,2,128]{2,1,0:T(2,128)}), f32[32,2,128]{2,1,0:T(2,128)S(1)}, u32[]{:S(2)}, u32[]{:S(2)}) async-start(f32[32,2,128]{2,1,0:T(2,128)} %bitcast.13), calls=%async_computation | async-start | bytes 65536 | tf_op jit(solution)/shard_map/all_to_all | solution.py:712
  29.3 0.0 copy-start.2
  29.3 5.1 %collective-permute-start.3 = (f32[11,8,128]{2,1,0:T(8,128)S(1)}, f32[11,8,128]{2,1,0:T(8,128)S(1)}, u32[]{:S(2)}, u32[]{:S(2)}) collective-permute-start(f32[11,8,128]{2,1,0:T(8,128)S(1)} %get-tuple-element.33), channel_id=1, source_target_pairs={{4,488},{12,496},{20,504},{484,8},{492,16},{500,24},{488,4},{496,1... | collective-permute-start | bytes 135176 | tf_op jit(solution)/shard_map/ppermute | solution.py:708
  34.4 1.3 %collective-permute-start.1 = (f32[33,8,128]{2,1,0:T(8,128)S(1)}, f32[33,8,128]{2,1,0:T(8,128)S(1)}, u32[]{:S(2)}, u32[]{:S(2)}) collective-permute-start(f32[33,8,128]{2,1,0:T(8,128)S(1)} %slice_bitcast_fusion), channel_id=1, source_target_pairs={{0,8},{8,16},{16,24},{12,4},{20,12},{28,20},{1,9},{9,17},{17,25},{... | collective-permute-start | bytes 405512 | tf_op jit(solution)/shard_map/ppermute | solution.py:724
  35.7 13.8 %collective-permute-start.4 = (f32[33,8,128]{2,1,0:T(8,128)S(1)}, f32[33,8,128]{2,1,0:T(8,128)S(1)}, u32[]{:S(2)}, u32[]{:S(2)}) collective-permute-start(f32[33,8,128]{2,1,0:T(8,128)S(1)} %pad_maximum_fusion), channel_id=1, source_target_pairs={{484,0},{480,4},{0,484},{4,480},{485,1},{481,5},{1,485},{5,481},{4... | collective-permute-start | bytes 405512 | tf_op jit(solution)/shard_map/ppermute | solution.py:714
  49.5 2.9 %all-to-all-done.arr = f32[32,2,128]{2,1,0:T(2,128)S(1)} async-done(((f32[32,2,128]{2,1,0:T(2,128)}), f32[32,2,128]{2,1,0:T(2,128)S(1)}, u32[]{:S(2)}, u32[]{:S(2)}) %all-to-all-start) | async-done | bytes 32800 | tf_op jit(solution)/shard_map/all_to_all | solution.py:712
  52.4 1.3 %collective-permute-start.2 = (f32[4,8,128]{2,1,0:T(8,128)S(1)}, f32[4,8,128]{2,1,0:T(8,128)S(1)}, u32[]{:S(2)}, u32[]{:S(2)}) collective-permute-start(f32[4,8,128]{2,1,0:T(8,128)S(1)} %bitcast.27), channel_id=1, source_target_pairs={{0,8},{8,16},{16,24},{12,4},{20,12},{28,20},{1,9},{9,17},{17,25},{... | collective-permute-start | bytes 49160 | tf_op jit(solution)/shard_map/ppermute | solution.py:726
  53.7 4.3 %collective-permute-done.2.third_in = f32[4,8,128]{2,1,0:T(8,128)S(1)} collective-permute-done((f32[4,8,128]{2,1,0:T(8,128)S(1)}, f32[4,8,128]{2,1,0:T(8,128)S(1)}, u32[]{:S(2)}, u32[]{:S(2)}) %collective-permute-start.2) | collective-permute-done | bytes 16416 | tf_op jit(solution)/shard_map/ppermute | solution.py:726
  58.1 0.0 collective-permute-done.1.fwd
  58.1 2.5 %deposit.1 = (f32[4,31,16,128]{3,2,1,0:T(8,128)S(1)}, f32[69,8,128]{2,1,0:T(8,128)S(1)}, f32[69,8,128]{2,1,0:T(8,128)S(1)}, f32[8,27,8,128]{3,2,1,0:T(8,128)S(1)}) custom-call(s32[9]{0:T(128)S(1)} %stack.63.sc, f32[27,4,8,128]{3,2,1,0:T(8,128)S(1)} %copy-done.2, s32[4,8,128]{2,1,0:T(8,128)S(1)} %copy-done.3, f32[3,4,8,128]{3,2,1,0:T(8,128)S(1)} %get-tuple-element.16.vel, ...), custom_call_target="tpu_custom_call" | custom-call | flops 49999998976 | bytes 1 | tf_op jit(solution)/shard_map/deposit/pallas_call | solution.py:644
  60.6 0.7 collective-permute-start.5
  61.3 1.9 %collective-permute-start.6 = (f32[69,8,128]{2,1,0:T(8,128)S(1)}, f32[69,8,128]{2,1,0:T(8,128)S(1)}, u32[]{:S(2)}, u32[]{:S(2)}) collective-permute-start(f32[69,8,128]{2,1,0:T(8,128)S(1)} %get-tuple-element.23), channel_id=1, source_target_pairs={{0,32},{32,0},{64,96},{96,64},{128,160},{160,128},{192,224},{224,1... | collective-permute-start | bytes 847880 | tf_op jit(solution)/shard_map/ppermute | solution.py:747
  63.3 1.5 %collective-permute-done.6.xar = f32[69,8,128]{2,1,0:T(8,128)S(1)} collective-permute-done((f32[69,8,128]{2,1,0:T(8,128)S(1)}, f32[69,8,128]{2,1,0:T(8,128)S(1)}, u32[]{:S(2)}, u32[]{:S(2)}) %collective-permute-start.6) | collective-permute-done | bytes 282656 | tf_op jit(solution)/shard_map/ppermute | solution.py:747
  64.8 2.2 %columns.1 = (f32[8,8,128]{2,1,0:T(8,128)S(1)}, f32[8,8,128]{2,1,0:T(8,128)S(1)}, f32[18,8,128]{2,1,0:T(8,128)S(1)}, f32[5,8,128]{2,1,0:T(8,128)S(1)}, f32[8,128]{1,0:T(8,128)S(1)}) custom-call(s32[9]{0:T(128)S(1)} %stack.63.sc, f32[4,31,16,128]{3,2,1,0:T(8,128)S(1)} %get-tuple-element.21.ye, f32[69,8,128]{2,1,0:T(8,128)S(1)} %collective-permute-done.5.xbr, ...), custom_call_target="tpu_custom_call" | custom-call | tf_op jit(solution)/shard_map/columns/pallas_call | solution.py:644
  67.0 3.1 %collective-permute-start.7 = (f32[8,8,128]{2,1,0:T(8,128)S(1)}, f32[8,8,128]{2,1,0:T(8,128)S(1)}, u32[]{:S(2)}, u32[]{:S(2)}) collective-permute-start(f32[8,8,128]{2,1,0:T(8,128)S(1)} %get-tuple-element.28), channel_id=1, source_target_pairs={{0,1},{1,0},{2,3},{3,2},{4,5},{5,4},{6,7},{7,6},{8,9},{9,8},{10,11... | collective-permute-start | bytes 98312 | tf_op jit(solution)/shard_map/ppermute | solution.py:765
  70.1 1.9 %collective-permute-start.8 = (f32[8,8,128]{2,1,0:T(8,128)S(1)}, f32[8,8,128]{2,1,0:T(8,128)S(1)}, u32[]{:S(2)}, u32[]{:S(2)}) collective-permute-start(f32[8,8,128]{2,1,0:T(8,128)S(1)} %get-tuple-element.29), channel_id=1, source_target_pairs={{1,2},{2,1},{5,6},{6,5},{9,10},{10,9},{13,14},{14,13},{17,18},{18,... | collective-permute-start | bytes 98312 | tf_op jit(solution)/shard_map/ppermute | solution.py:767
  72.1 0.8 collective-permute-done.7.zar
  72.8 3.1 %collective-permute-done.8.zbr = f32[8,8,128]{2,1,0:T(8,128)S(1)} collective-permute-done((f32[8,8,128]{2,1,0:T(8,128)S(1)}, f32[8,8,128]{2,1,0:T(8,128)S(1)}, u32[]{:S(2)}, u32[]{:S(2)}) %collective-permute-start.8) | collective-permute-done | bytes 32800 | tf_op jit(solution)/shard_map/ppermute | solution.py:767
  76.0 6.6 %steps.1 = (f32[27,4,8,128]{3,2,1,0:T(8,128)}, f32[27,8,4,64]{3,2,1,0:T(4,128)}) custom-call(s32[9]{0:T(128)S(1)} %stack.63.sc, f32[4,31,16,128]{3,2,1,0:T(8,128)S(1)} %get-tuple-element.21.ye, f32[69,8,128]{2,1,0:T(8,128)S(1)} %collective-permute-done.5.xbr, f32[69,8,128]{2,1,0:T(8,128)S(1)} %collective-permute-done.6.xar, ...), custom_call_target="tpu_custom_call" | custom-call | tf_op jit(solution)/shard_map/steps/pallas_call | solution.py:644
  (21 shorter events, 0.1 us)
Async XLA Ops:
  0.7 0.7 copy-start.3
  0.7 0.7 copy-start.4
  1.4 1.0 %copy-start = (f32[27,8,4,64]{3,2,1,0:T(4,128)S(1)}, f32[27,8,4,64]{3,2,1,0:T(4,128)}, u32[]{:S(2)}) copy-start(f32[27,8,4,64]{3,2,1,0:T(4,128)} %cpop.1) | copy-start | bytes 663556
  2.4 1.0 %copy-start.1 = (f32[27,4,8,128]{3,2,1,0:T(8,128)S(1)}, f32[27,4,8,128]{3,2,1,0:T(8,128)}, u32[]{:S(2)}) copy-start(f32[27,4,8,128]{3,2,1,0:T(8,128)} %pop.3) | copy-start | bytes 1327108
  3.4 17.9 %copy-start.8 = (f32[1,1,1,3,256]{4,2,3,1,0:T(1,128)S(1)}, f32[1,1,1,3,256]{4,2,3,1,0:T(1,128)}, u32[]{:S(2)}) copy-start(f32[1,1,1,3,256]{4,2,3,1,0:T(1,128)} %param.15) | copy-start | bytes 9220
  5.5 15.9 %copy-start.9 = (f32[1,1,1,3,256]{4,2,3,1,0:T(1,128)S(1)}, f32[1,1,1,3,256]{4,2,3,1,0:T(1,128)}, u32[]{:S(2)}) copy-start(f32[1,1,1,3,256]{4,2,3,1,0:T(1,128)} %param.16) | copy-start | bytes 9220
  5.5 28.9 %collective-permute-start = (f32[2,33,8,128]{3,2,1,0:T(8,128)S(1)}, f32[2,33,8,128]{3,2,1,0:T(8,128)S(1)}, u32[]{:S(2)}, u32[]{:S(2)}) collective-permute-start(f32[2,33,8,128]{3,2,1,0:T(8,128)S(1)} %get-tuple-element.18), channel_id=1, source_target_pairs={{0,4},{4,0},{1,5},{5,1},{2,6},{6,2},{3,7},{7,3},{8,12},{12,8},{9,1... | collective-permute-start | bytes 811016 | tf_op jit(solution)/shard_map/ppermute | solution.py:711
  21.4 0.7 copy-start.6
  21.4 0.7 copy-start.7
  21.4 0.7 copy-start.5
  23.8 28.6 %all-to-all-start = ((f32[32,2,128]{2,1,0:T(2,128)}), f32[32,2,128]{2,1,0:T(2,128)S(1)}, u32[]{:S(2)}, u32[]{:S(2)}) async-start(f32[32,2,128]{2,1,0:T(2,128)} %bitcast.13), calls=%async_computation | async-start | bytes 65536 | tf_op jit(solution)/shard_map/all_to_all | solution.py:712
  29.3 28.8 %copy-start.2 = (f32[27,4,8,128]{3,2,1,0:T(8,128)S(1)}, f32[27,4,8,128]{3,2,1,0:T(8,128)}, u32[]{:S(2)}) copy-start(f32[27,4,8,128]{3,2,1,0:T(8,128)} %pop.3) | copy-start | bytes 1327108
  29.3 24.4 %collective-permute-start.3 = (f32[11,8,128]{2,1,0:T(8,128)S(1)}, f32[11,8,128]{2,1,0:T(8,128)S(1)}, u32[]{:S(2)}, u32[]{:S(2)}) collective-permute-start(f32[11,8,128]{2,1,0:T(8,128)S(1)} %get-tuple-element.33), channel_id=1, source_target_pairs={{4,488},{12,496},{20,504},{484,8},{492,16},{500,24},{488,4},{496,1... | collective-permute-start | bytes 135176 | tf_op jit(solution)/shard_map/ppermute | solution.py:708
  34.4 23.7 %collective-permute-start.1 = (f32[33,8,128]{2,1,0:T(8,128)S(1)}, f32[33,8,128]{2,1,0:T(8,128)S(1)}, u32[]{:S(2)}, u32[]{:S(2)}) collective-permute-start(f32[33,8,128]{2,1,0:T(8,128)S(1)} %slice_bitcast_fusion), channel_id=1, source_target_pairs={{0,8},{8,16},{16,24},{12,4},{20,12},{28,20},{1,9},{9,17},{17,25},{... | collective-permute-start | bytes 405512 | tf_op jit(solution)/shard_map/ppermute | solution.py:724
  35.7 22.3 %collective-permute-start.4 = (f32[33,8,128]{2,1,0:T(8,128)S(1)}, f32[33,8,128]{2,1,0:T(8,128)S(1)}, u32[]{:S(2)}, u32[]{:S(2)}) collective-permute-start(f32[33,8,128]{2,1,0:T(8,128)S(1)} %pad_maximum_fusion), channel_id=1, source_target_pairs={{484,0},{480,4},{0,484},{4,480},{485,1},{481,5},{1,485},{5,481},{4... | collective-permute-start | bytes 405512 | tf_op jit(solution)/shard_map/ppermute | solution.py:714
  52.4 5.6 %collective-permute-start.2 = (f32[4,8,128]{2,1,0:T(8,128)S(1)}, f32[4,8,128]{2,1,0:T(8,128)S(1)}, u32[]{:S(2)}, u32[]{:S(2)}) collective-permute-start(f32[4,8,128]{2,1,0:T(8,128)S(1)} %bitcast.27), channel_id=1, source_target_pairs={{0,8},{8,16},{16,24},{12,4},{20,12},{28,20},{1,9},{9,17},{17,25},{... | collective-permute-start | bytes 49160 | tf_op jit(solution)/shard_map/ppermute | solution.py:726
  60.6 2.6 %collective-permute-start.5 = (f32[69,8,128]{2,1,0:T(8,128)S(1)}, f32[69,8,128]{2,1,0:T(8,128)S(1)}, u32[]{:S(2)}, u32[]{:S(2)}) collective-permute-start(f32[69,8,128]{2,1,0:T(8,128)S(1)} %get-tuple-element.22), channel_id=1, source_target_pairs={{32,64},{96,128},{160,192},{224,256},{288,320},{352,384},{416,448}... | collective-permute-start | bytes 847880 | tf_op jit(solution)/shard_map/ppermute | solution.py:746
  61.3 3.5 %collective-permute-start.6 = (f32[69,8,128]{2,1,0:T(8,128)S(1)}, f32[69,8,128]{2,1,0:T(8,128)S(1)}, u32[]{:S(2)}, u32[]{:S(2)}) collective-permute-start(f32[69,8,128]{2,1,0:T(8,128)S(1)} %get-tuple-element.23), channel_id=1, source_target_pairs={{0,32},{32,0},{64,96},{96,64},{128,160},{160,128},{192,224},{224,1... | collective-permute-start | bytes 847880 | tf_op jit(solution)/shard_map/ppermute | solution.py:747
  67.0 5.8 %collective-permute-start.7 = (f32[8,8,128]{2,1,0:T(8,128)S(1)}, f32[8,8,128]{2,1,0:T(8,128)S(1)}, u32[]{:S(2)}, u32[]{:S(2)}) collective-permute-start(f32[8,8,128]{2,1,0:T(8,128)S(1)} %get-tuple-element.28), channel_id=1, source_target_pairs={{0,1},{1,0},{2,3},{3,2},{4,5},{5,4},{6,7},{7,6},{8,9},{9,8},{10,11... | collective-permute-start | bytes 98312 | tf_op jit(solution)/shard_map/ppermute | solution.py:765
  70.1 5.8 %collective-permute-start.8 = (f32[8,8,128]{2,1,0:T(8,128)S(1)}, f32[8,8,128]{2,1,0:T(8,128)S(1)}, u32[]{:S(2)}, u32[]{:S(2)}) collective-permute-start(f32[8,8,128]{2,1,0:T(8,128)S(1)} %get-tuple-element.29), channel_id=1, source_target_pairs={{1,2},{2,1},{5,6},{6,5},{9,10},{10,9},{13,14},{14,13},{17,18},{18,... | collective-permute-start | bytes 98312 | tf_op jit(solution)/shard_map/ppermute | solution.py:767

commit v4 on v3

--- a/solution.py
+++ b/solution.py
@@ -574,11 +574,13 @@
         within = within & (
             (lane256 < 128) | ((lane256 < 132) & has_zhi) | ((lane256 >= 252) & has_zlo)
         )
-        for layer, to in ((n127, p1.at[1]), (later, late)):
-            layer = interface(layer, prolong_factor)
-            fines = select(select(jnp.concatenate(layer, axis=0), wide), tall, left=True)
+        both = interface(n127, prolong_factor) + interface(later, prolong_factor)
+        spread = select(jnp.concatenate(both, axis=0), wide)
+        fines = select(jnp.concatenate([spread[0:216], spread[216:432]], axis=1), tall, left=True)
+        for k, to in enumerate((p1.at[1], late)):
             for i in range(27):
-                to[i] = jnp.where(within, fines[16 * i : 16 * i + 16], wall)
+                fine_layer = fines[16 * i : 16 * i + 16, 256 * k : 256 * k + 256]
+                to[i] = jnp.where(within, fine_layer, wall)
 
     @pl.when(last)
     def _():

time: 83 us -> 83.4 us (level)
  no operation moved by 1% of the time
where the time goes in v4:
time: 83.4 us; the launch traced here: 82.8 us
  starting transfers between devices  50.3 us (60%)
  Pallas kernels  15.5 us (19%)
  waiting for transfers between devices  12.6 us (15%)
  local copies, waits for them, and re-layouts  3.45 us (4%)
  between operations  0.92 us (1%)
    ppermute x1, starting transfers between devices, body(): near = lax.ppermute(faces, 'h', [(0, 1), (1, 0)])  15.8 us
    pallas_call x5, Pallas kernels, call(): pl.pallas_call(kernel, out_shape=out_shape, in_specs=[pl.BlockSpec(memory...  15.5 us
    ppermute x1, starting transfers between devices, body(): lax.ppermute(jnp.concatenate([near[0, T_LEVEL:T_FACE], near[1, T_LEVEL:T_...  13.8 us
    all_to_all x1, starting transfers between devices, body(): lax.all_to_all(outbox.reshape(2 * n_gx, 2, 128), ('gx', 'h'), 0, 0, tiled...  5.41 us
    ppermute x1, starting transfers between devices, body(): lax.ppermute(faces[1, T_LEVEL:T_FACE], ('gx', 'y', 'h'), far_ends + [(j,...  5.05 us
    ppermute x1, waiting for transfers between devices, body(): third = lax.ppermute(partner, ('y', 'h'), onward)  4.32 us
    unnamed x22, local copies, waits for them, and re-layouts  3.33 us
    ppermute x1, waiting for transfers between devices, body(): zbr = lax.ppermute(zb, 'gz', inner + [(j, i) for i, j in inner])  3.12 us
  transfers between devices with their start and end apart: 10, of which 5 were waited for; matrix products, arithmetic and copies ran while one was open for 0% of the time, Pallas kernels for 2%

profile of v4, /device:TPU:28, one launch (start us, length us, event | category | flops | bytes accessed | tf_op | source)
XLA Modules:
  0.0 82.8 jit_solution(1897473064624683004)
XLA Ops:
  0.7 0.1 stack.63.sc
  0.8 0.6 copy-done.3
  1.4 1.0 %copy-done = f32[27,8,4,64]{3,2,1,0:T(4,128)S(1)} copy-done((f32[27,8,4,64]{3,2,1,0:T(4,128)S(1)}, f32[27,8,4,64]{3,2,1,0:T(4,128)}, u32[]{:S(2)}) %copy-start) | copy-done | bytes 221208
  2.4 1.0 %copy-done.1 = f32[27,4,8,128]{3,2,1,0:T(8,128)S(1)} copy-done((f32[27,4,8,128]{3,2,1,0:T(8,128)S(1)}, f32[27,4,8,128]{3,2,1,0:T(8,128)}, u32[]{:S(2)}) %copy-start.1) | copy-done | bytes 442392
  3.4 2.1 %pack.1 = (f32[2,33,8,128]{3,2,1,0:T(8,128)S(1)}, f32[3,4,8,128]{3,2,1,0:T(8,128)S(1)}, f32[8,27,8,128]{3,2,1,0:T(8,128)S(1)}, f32[27,8,128]{2,1,0:T(8,128)}, f32[9,8,128]{2,1,0:T(8,128)S(1)}) custom-call(s32[9]{0:T(128)S(1)} %stack.63.sc, f32[27,4,8,128]{3,2,1,0:T(8,128)S(1)} %copy-done.1, f32[27,8,4,64]{3,2,1,0:T(4,128)S(1)} %copy-done, ...), custom_call_target="tpu_custom_call" | custom-call | tf_op jit(solution)/shard_map/pack/pallas_call | solution.py:646
  5.5 15.8 %collective-permute-start = (f32[2,33,8,128]{3,2,1,0:T(8,128)S(1)}, f32[2,33,8,128]{3,2,1,0:T(8,128)S(1)}, u32[]{:S(2)}, u32[]{:S(2)}) collective-permute-start(f32[2,33,8,128]{3,2,1,0:T(8,128)S(1)} %get-tuple-element.18), channel_id=1, source_target_pairs={{0,4},{4,0},{1,5},{5,1},{2,6},{6,2},{3,7},{7,3},{8,12},{12,8},{9,1... | collective-permute-start | bytes 811016 | tf_op jit(solution)/shard_map/ppermute | solution.py:713
  21.4 0.0 copy-start.6
  21.4 0.0 copy-start.7
  21.4 0.0 copy-start.5
  21.4 0.6 copy-done.6
  22.1 0.0 copy-done.7
  22.1 0.0 copy-done.5
  22.1 1.8 %route.1 = f32[64,128]{1,0:T(8,128)} custom-call(s32[9]{0:T(128)S(1)} %stack.63.sc, s32[1,256]{1,0:T(1,128)S(1)} %bitcast.24, s32[1,256]{1,0:T(1,128)S(1)} %bitcast.25, f32[1,1,1,3,256]{4,3,2,1,0:T(4,128)S(1)} %copy.11.pvel, f32[1,1,1,3,256]{4,3,2,1,0:T(4,128)S(1)} %copy.12.pfrac, f32[1,256]{1,0:T(1,128)S(1)} %bitcast.26, ...), custom_call_target="tpu_custom_call" | custom-call | flops 49999998976 | bytes 1 | tf_op jit(solution)/shard_map/route/pallas_call | solution.py:646
  23.8 5.4 %all-to-all-start = ((f32[32,2,128]{2,1,0:T(2,128)}), f32[32,2,128]{2,1,0:T(2,128)S(1)}, u32[]{:S(2)}, u32[]{:S(2)}) async-start(f32[32,2,128]{2,1,0:T(2,128)} %bitcast.13), calls=%async_computation | async-start | bytes 65536 | tf_op jit(solution)/shard_map/all_to_all | solution.py:714
  29.3 0.0 copy-start.2
  29.3 5.1 %collective-permute-start.3 = (f32[11,8,128]{2,1,0:T(8,128)S(1)}, f32[11,8,128]{2,1,0:T(8,128)S(1)}, u32[]{:S(2)}, u32[]{:S(2)}) collective-permute-start(f32[11,8,128]{2,1,0:T(8,128)S(1)} %get-tuple-element.33), channel_id=1, source_target_pairs={{4,488},{12,496},{20,504},{484,8},{492,16},{500,24},{488,4},{496,1... | collective-permute-start | bytes 135176 | tf_op jit(solution)/shard_map/ppermute | solution.py:710
  34.4 1.3 %collective-permute-start.1 = (f32[33,8,128]{2,1,0:T(8,128)S(1)}, f32[33,8,128]{2,1,0:T(8,128)S(1)}, u32[]{:S(2)}, u32[]{:S(2)}) collective-permute-start(f32[33,8,128]{2,1,0:T(8,128)S(1)} %slice_bitcast_fusion), channel_id=1, source_target_pairs={{0,8},{8,16},{16,24},{12,4},{20,12},{28,20},{1,9},{9,17},{17,25},{... | collective-permute-start | bytes 405512 | tf_op jit(solution)/shard_map/ppermute | solution.py:726
  35.7 13.8 %collective-permute-start.4 = (f32[33,8,128]{2,1,0:T(8,128)S(1)}, f32[33,8,128]{2,1,0:T(8,128)S(1)}, u32[]{:S(2)}, u32[]{:S(2)}) collective-permute-start(f32[33,8,128]{2,1,0:T(8,128)S(1)} %pad_maximum_fusion), channel_id=1, source_target_pairs={{484,0},{480,4},{0,484},{4,480},{485,1},{481,5},{1,485},{5,481},{4... | collective-permute-start | bytes 405512 | tf_op jit(solution)/shard_map/ppermute | solution.py:716
  49.5 2.9 %all-to-all-done.arr = f32[32,2,128]{2,1,0:T(2,128)S(1)} async-done(((f32[32,2,128]{2,1,0:T(2,128)}), f32[32,2,128]{2,1,0:T(2,128)S(1)}, u32[]{:S(2)}, u32[]{:S(2)}) %all-to-all-start) | async-done | bytes 32800 | tf_op jit(solution)/shard_map/all_to_all | solution.py:714
  52.4 1.3 %collective-permute-start.2 = (f32[4,8,128]{2,1,0:T(8,128)S(1)}, f32[4,8,128]{2,1,0:T(8,128)S(1)}, u32[]{:S(2)}, u32[]{:S(2)}) collective-permute-start(f32[4,8,128]{2,1,0:T(8,128)S(1)} %bitcast.27), channel_id=1, source_target_pairs={{0,8},{8,16},{16,24},{12,4},{20,12},{28,20},{1,9},{9,17},{17,25},{... | collective-permute-start | bytes 49160 | tf_op jit(solution)/shard_map/ppermute | solution.py:728
  53.7 4.3 %collective-permute-done.2.third_in = f32[4,8,128]{2,1,0:T(8,128)S(1)} collective-permute-done((f32[4,8,128]{2,1,0:T(8,128)S(1)}, f32[4,8,128]{2,1,0:T(8,128)S(1)}, u32[]{:S(2)}, u32[]{:S(2)}) %collective-permute-start.2) | collective-permute-done | bytes 16416 | tf_op jit(solution)/shard_map/ppermute | solution.py:728
  58.1 0.0 collective-permute-done.1.fwd
  58.1 2.5 %deposit.1 = (f32[4,31,16,128]{3,2,1,0:T(8,128)S(1)}, f32[69,8,128]{2,1,0:T(8,128)S(1)}, f32[69,8,128]{2,1,0:T(8,128)S(1)}, f32[8,27,8,128]{3,2,1,0:T(8,128)S(1)}) custom-call(s32[9]{0:T(128)S(1)} %stack.63.sc, f32[27,4,8,128]{3,2,1,0:T(8,128)S(1)} %copy-done.2, s32[4,8,128]{2,1,0:T(8,128)S(1)} %copy-done.3, f32[3,4,8,128]{3,2,1,0:T(8,128)S(1)} %get-tuple-element.16.vel, ...), custom_call_target="tpu_custom_call" | custom-call | flops 49999998976 | bytes 1 | tf_op jit(solution)/shard_map/deposit/pallas_call | solution.py:646
  60.6 0.7 collective-permute-start.5
  61.3 1.9 %collective-permute-start.6 = (f32[69,8,128]{2,1,0:T(8,128)S(1)}, f32[69,8,128]{2,1,0:T(8,128)S(1)}, u32[]{:S(2)}, u32[]{:S(2)}) collective-permute-start(f32[69,8,128]{2,1,0:T(8,128)S(1)} %get-tuple-element.23), channel_id=1, source_target_pairs={{0,32},{32,0},{64,96},{96,64},{128,160},{160,128},{192,224},{224,1... | collective-permute-start | bytes 847880 | tf_op jit(solution)/shard_map/ppermute | solution.py:749
  63.3 1.5 %collective-permute-done.6.xar = f32[69,8,128]{2,1,0:T(8,128)S(1)} collective-permute-done((f32[69,8,128]{2,1,0:T(8,128)S(1)}, f32[69,8,128]{2,1,0:T(8,128)S(1)}, u32[]{:S(2)}, u32[]{:S(2)}) %collective-permute-start.6) | collective-permute-done | bytes 282656 | tf_op jit(solution)/shard_map/ppermute | solution.py:749
  64.8 2.2 %columns.1 = (f32[8,8,128]{2,1,0:T(8,128)S(1)}, f32[8,8,128]{2,1,0:T(8,128)S(1)}, f32[18,8,128]{2,1,0:T(8,128)S(1)}, f32[5,8,128]{2,1,0:T(8,128)S(1)}, f32[8,128]{1,0:T(8,128)S(1)}) custom-call(s32[9]{0:T(128)S(1)} %stack.63.sc, f32[4,31,16,128]{3,2,1,0:T(8,128)S(1)} %get-tuple-element.21.ye, f32[69,8,128]{2,1,0:T(8,128)S(1)} %collective-permute-done.5.xbr, ...), custom_call_target="tpu_custom_call" | custom-call | tf_op jit(solution)/shard_map/columns/pallas_call | solution.py:646
  67.0 3.1 %collective-permute-start.7 = (f32[8,8,128]{2,1,0:T(8,128)S(1)}, f32[8,8,128]{2,1,0:T(8,128)S(1)}, u32[]{:S(2)}, u32[]{:S(2)}) collective-permute-start(f32[8,8,128]{2,1,0:T(8,128)S(1)} %get-tuple-element.28), channel_id=1, source_target_pairs={{0,1},{1,0},{2,3},{3,2},{4,5},{5,4},{6,7},{7,6},{8,9},{9,8},{10,11... | collective-permute-start | bytes 98312 | tf_op jit(solution)/shard_map/ppermute | solution.py:767
  70.1 1.9 %collective-permute-start.8 = (f32[8,8,128]{2,1,0:T(8,128)S(1)}, f32[8,8,128]{2,1,0:T(8,128)S(1)}, u32[]{:S(2)}, u32[]{:S(2)}) collective-permute-start(f32[8,8,128]{2,1,0:T(8,128)S(1)} %get-tuple-element.29), channel_id=1, source_target_pairs={{1,2},{2,1},{5,6},{6,5},{9,10},{10,9},{13,14},{14,13},{17,18},{18,... | collective-permute-start | bytes 98312 | tf_op jit(solution)/shard_map/ppermute | solution.py:769
  72.1 0.8 collective-permute-done.7.zar
  72.8 3.1 %collective-permute-done.8.zbr = f32[8,8,128]{2,1,0:T(8,128)S(1)} collective-permute-done((f32[8,8,128]{2,1,0:T(8,128)S(1)}, f32[8,8,128]{2,1,0:T(8,128)S(1)}, u32[]{:S(2)}, u32[]{:S(2)}) %collective-permute-start.8) | collective-permute-done | bytes 32800 | tf_op jit(solution)/shard_map/ppermute | solution.py:769
  76.0 6.9 %steps.1 = (f32[27,4,8,128]{3,2,1,0:T(8,128)}, f32[27,8,4,64]{3,2,1,0:T(4,128)}) custom-call(s32[9]{0:T(128)S(1)} %stack.63.sc, f32[4,31,16,128]{3,2,1,0:T(8,128)S(1)} %get-tuple-element.21.ye, f32[69,8,128]{2,1,0:T(8,128)S(1)} %collective-permute-done.5.xbr, f32[69,8,128]{2,1,0:T(8,128)S(1)} %collective-permute-done.6.xar, ...), custom_call_target="tpu_custom_call" | custom-call | tf_op jit(solution)/shard_map/steps/pallas_call | solution.py:646
  (21 shorter events, 0.1 us)
Async XLA Ops:
  0.7 0.7 copy-start.3
  0.7 0.7 copy-start.4
  1.4 1.0 %copy-start = (f32[27,8,4,64]{3,2,1,0:T(4,128)S(1)}, f32[27,8,4,64]{3,2,1,0:T(4,128)}, u32[]{:S(2)}) copy-start(f32[27,8,4,64]{3,2,1,0:T(4,128)} %cpop.1) | copy-start | bytes 663556
  2.4 1.0 %copy-start.1 = (f32[27,4,8,128]{3,2,1,0:T(8,128)S(1)}, f32[27,4,8,128]{3,2,1,0:T(8,128)}, u32[]{:S(2)}) copy-start(f32[27,4,8,128]{3,2,1,0:T(8,128)} %pop.3) | copy-start | bytes 1327108
  3.4 17.9 %copy-start.8 = (f32[1,1,1,3,256]{4,2,3,1,0:T(1,128)S(1)}, f32[1,1,1,3,256]{4,2,3,1,0:T(1,128)}, u32[]{:S(2)}) copy-start(f32[1,1,1,3,256]{4,2,3,1,0:T(1,128)} %param.15) | copy-start | bytes 9220
  5.5 15.9 %copy-start.9 = (f32[1,1,1,3,256]{4,2,3,1,0:T(1,128)S(1)}, f32[1,1,1,3,256]{4,2,3,1,0:T(1,128)}, u32[]{:S(2)}) copy-start(f32[1,1,1,3,256]{4,2,3,1,0:T(1,128)} %param.16) | copy-start | bytes 9220
  5.5 28.9 %collective-permute-start = (f32[2,33,8,128]{3,2,1,0:T(8,128)S(1)}, f32[2,33,8,128]{3,2,1,0:T(8,128)S(1)}, u32[]{:S(2)}, u32[]{:S(2)}) collective-permute-start(f32[2,33,8,128]{3,2,1,0:T(8,128)S(1)} %get-tuple-element.18), channel_id=1, source_target_pairs={{0,4},{4,0},{1,5},{5,1},{2,6},{6,2},{3,7},{7,3},{8,12},{12,8},{9,1... | collective-permute-start | bytes 811016 | tf_op jit(solution)/shard_map/ppermute | solution.py:713
  21.4 0.7 copy-start.6
  21.4 0.7 copy-start.7
  21.4 0.7 copy-start.5
  23.8 28.6 %all-to-all-start = ((f32[32,2,128]{2,1,0:T(2,128)}), f32[32,2,128]{2,1,0:T(2,128)S(1)}, u32[]{:S(2)}, u32[]{:S(2)}) async-start(f32[32,2,128]{2,1,0:T(2,128)} %bitcast.13), calls=%async_computation | async-start | bytes 65536 | tf_op jit(solution)/shard_map/all_to_all | solution.py:714
  29.3 28.8 %copy-start.2 = (f32[27,4,8,128]{3,2,1,0:T(8,128)S(1)}, f32[27,4,8,128]{3,2,1,0:T(8,128)}, u32[]{:S(2)}) copy-start(f32[27,4,8,128]{3,2,1,0:T(8,128)} %pop.3) | copy-start | bytes 1327108
  29.3 24.4 %collective-permute-start.3 = (f32[11,8,128]{2,1,0:T(8,128)S(1)}, f32[11,8,128]{2,1,0:T(8,128)S(1)}, u32[]{:S(2)}, u32[]{:S(2)}) collective-permute-start(f32[11,8,128]{2,1,0:T(8,128)S(1)} %get-tuple-element.33), channel_id=1, source_target_pairs={{4,488},{12,496},{20,504},{484,8},{492,16},{500,24},{488,4},{496,1... | collective-permute-start | bytes 135176 | tf_op jit(solution)/shard_map/ppermute | solution.py:710
  34.4 23.7 %collective-permute-start.1 = (f32[33,8,128]{2,1,0:T(8,128)S(1)}, f32[33,8,128]{2,1,0:T(8,128)S(1)}, u32[]{:S(2)}, u32[]{:S(2)}) collective-permute-start(f32[33,8,128]{2,1,0:T(8,128)S(1)} %slice_bitcast_fusion), channel_id=1, source_target_pairs={{0,8},{8,16},{16,24},{12,4},{20,12},{28,20},{1,9},{9,17},{17,25},{... | collective-permute-start | bytes 405512 | tf_op jit(solution)/shard_map/ppermute | solution.py:726
  35.7 22.3 %collective-permute-start.4 = (f32[33,8,128]{2,1,0:T(8,128)S(1)}, f32[33,8,128]{2,1,0:T(8,128)S(1)}, u32[]{:S(2)}, u32[]{:S(2)}) collective-permute-start(f32[33,8,128]{2,1,0:T(8,128)S(1)} %pad_maximum_fusion), channel_id=1, source_target_pairs={{484,0},{480,4},{0,484},{4,480},{485,1},{481,5},{1,485},{5,481},{4... | collective-permute-start | bytes 405512 | tf_op jit(solution)/shard_map/ppermute | solution.py:716
  52.4 5.6 %collective-permute-start.2 = (f32[4,8,128]{2,1,0:T(8,128)S(1)}, f32[4,8,128]{2,1,0:T(8,128)S(1)}, u32[]{:S(2)}, u32[]{:S(2)}) collective-permute-start(f32[4,8,128]{2,1,0:T(8,128)S(1)} %bitcast.27), channel_id=1, source_target_pairs={{0,8},{8,16},{16,24},{12,4},{20,12},{28,20},{1,9},{9,17},{17,25},{... | collective-permute-start | bytes 49160 | tf_op jit(solution)/shard_map/ppermute | solution.py:728
  60.6 2.6 %collective-permute-start.5 = (f32[69,8,128]{2,1,0:T(8,128)S(1)}, f32[69,8,128]{2,1,0:T(8,128)S(1)}, u32[]{:S(2)}, u32[]{:S(2)}) collective-permute-start(f32[69,8,128]{2,1,0:T(8,128)S(1)} %get-tuple-element.22), channel_id=1, source_target_pairs={{32,64},{96,128},{160,192},{224,256},{288,320},{352,384},{416,448}... | collective-permute-start | bytes 847880 | tf_op jit(solution)/shard_map/ppermute | solution.py:748
  61.3 3.5 %collective-permute-start.6 = (f32[69,8,128]{2,1,0:T(8,128)S(1)}, f32[69,8,128]{2,1,0:T(8,128)S(1)}, u32[]{:S(2)}, u32[]{:S(2)}) collective-permute-start(f32[69,8,128]{2,1,0:T(8,128)S(1)} %get-tuple-element.23), channel_id=1, source_target_pairs={{0,32},{32,0},{64,96},{96,64},{128,160},{160,128},{192,224},{224,1... | collective-permute-start | bytes 847880 | tf_op jit(solution)/shard_map/ppermute | solution.py:749
  67.0 5.8 %collective-permute-start.7 = (f32[8,8,128]{2,1,0:T(8,128)S(1)}, f32[8,8,128]{2,1,0:T(8,128)S(1)}, u32[]{:S(2)}, u32[]{:S(2)}) collective-permute-start(f32[8,8,128]{2,1,0:T(8,128)S(1)} %get-tuple-element.28), channel_id=1, source_target_pairs={{0,1},{1,0},{2,3},{3,2},{4,5},{5,4},{6,7},{7,6},{8,9},{9,8},{10,11... | collective-permute-start | bytes 98312 | tf_op jit(solution)/shard_map/ppermute | solution.py:767
  70.1 5.8 %collective-permute-start.8 = (f32[8,8,128]{2,1,0:T(8,128)S(1)}, f32[8,8,128]{2,1,0:T(8,128)S(1)}, u32[]{:S(2)}, u32[]{:S(2)}) collective-permute-start(f32[8,8,128]{2,1,0:T(8,128)S(1)} %get-tuple-element.29), channel_id=1, source_target_pairs={{1,2},{2,1},{5,6},{6,5},{9,10},{10,9},{13,14},{14,13},{17,18},{18,... | collective-permute-start | bytes 98312 | tf_op jit(solution)/shard_map/ppermute | solution.py:769
